TPU v7x, 32 devices: a whole 2x2x4 slice. The times are simulated.
32 devices in a mesh: replica: 8 (over z, x), shard: 4 (over y, core).
Axes of the slice: x: 2, y: 2, z: 4, core: 2. Of those that a mesh axis runs over, the one named last changes fastest.
Arguments:
- tokens: bfloat16 [4096, 768], P(('replica', 'shard')), may hold values from -6 to 6
- cotangent: bfloat16 [4096, 768], P(('replica', 'shard')), may hold values from -6 to 6
- seq_lengths: int32 [32, 4], P(('replica', 'shard')), may hold values from 1 to 96, 128 in all within a row
- w_in: bfloat16 [768, 3352], P('shard'), may hold values from -0.21875 to 0.21875
- w_out: bfloat16 [1536, 768], P('shard'), may hold values from -0.15625 to 0.15625
- w_small: bfloat16 [11336], P('shard')
- m_in: float32 [768, 3352], P('shard'), may hold values from -6 to 6
- v_in: float32 [768, 3352], P('shard'), may hold values from 18.432 to 73.728
- m_out: float32 [1536, 768], P('shard'), may hold values from -28 to 28
- v_out: float32 [1536, 768], P('shard'), may hold values from 102.4 to 409.6
- m_small: float32 [11336], P('shard'), may hold values from -20 to 20
- v_small: float32 [11336], P('shard'), may hold values from 51.2 to 204.8
Outputs:
- block_out: bfloat16 [4096, 768], P(('replica', 'shard'))
- grad_tokens: bfloat16 [4096, 768], P(('replica', 'shard'))
- new_w_in: float32 [768, 3352], P('shard')
- new_m_in: float32 [768, 3352], P('shard')
- new_v_in: float32 [768, 3352], P('shard')
- new_w_out: float32 [1536, 768], P('shard')
- new_m_out: float32 [1536, 768], P('shard')
- new_v_out: float32 [1536, 768], P('shard')
- new_w_small: float32 [11336], P('shard')
- new_m_small: float32 [11336], P('shard')
- new_v_small: float32 [11336], P('shard')
Inputs may be any that keep to these rules, and one draw needn't show every extreme that they name: `seq_lengths`: in each row the first 3 entries are sequence lengths and the last is the padding at the block's end; each row sums to 128 and its largest entry is 96.
All inputs are finite; a program needn't handle non-finite values.
Results may differ from a plain program's by a relative error of at most 0.0094.
Values may be sent and summed in bfloat16 or wider, within the bound.
A program may use at most 128 MiB of HBM per device.

v0:
```python
import jax
import jax.numpy as jnp
from jax import lax
from jax.sharding import PartitionSpec as P

D = 768
STATE = 128
HEAD = 64
KCONV = 4
STEP = 10
DI = 1536


epsilon = 1e-05
beta_one = 0.9
beta_two = 0.95
adam_eps = 1e-08


def make_rounders():

    def round_plain(value):
        return lax.optimization_barrier(value.astype(jnp.bfloat16)).astype(jnp.float32)

    def unchanged(value):
        return value

    round_value = jax.custom_vjp(round_plain)
    round_grad = jax.custom_vjp(unchanged)

    def value_keep(value):
        return (round_plain(value), None)

    def value_pass(kept, gradient):
        return (gradient,)

    def grad_keep(value):
        return (value, None)

    def grad_round(kept, gradient):
        return (round_plain(gradient),)

    round_value.defvjp(value_keep, value_pass)
    round_grad.defvjp(grad_keep, grad_round)
    return (round_value, round_grad)


def mixer(resid, weight_in, weight_out, packed, seglens, round_value, round_grad):
    rows_count = resid.shape[0]
    channels = DI + 2 * STATE
    heads = DI // HEAD
    kernel = packed[: KCONV * channels].reshape(KCONV, channels)
    conv_bias = packed[KCONV * channels : (KCONV + 1) * channels]
    start = (KCONV + 1) * channels
    step_bias = packed[start : start + heads]
    decay_log = packed[start + heads : start + 2 * heads]
    skip_gain = packed[start + 2 * heads : start + 3 * heads]
    pre_gain = packed[start + 3 * heads : start + 3 * heads + D]
    gate_gain = packed[start + 3 * heads + D :]
    places = jnp.arange(rows_count, dtype=jnp.int32)
    bounds = jnp.cumsum(seglens)
    segment = jnp.sum((places[:, None] >= bounds[None, :]).astype(jnp.int32), axis=1)
    meansq = jnp.mean(resid * resid, axis=1, keepdims=True)
    normed = resid * lax.rsqrt(meansq + epsilon) * pre_gain
    project = round_grad(
        jnp.dot(round_value(normed), weight_in, preferred_element_type=jnp.float32)
    )
    gate_raw = project[:, :DI]
    conv_in = project[:, DI : DI + channels]
    step_raw = project[:, DI + channels :]
    convolved = conv_bias + kernel[KCONV - 1] * conv_in
    for offset in range(1, KCONV):
        shifted = jnp.concatenate(
            [jnp.zeros((offset, channels), jnp.float32), conv_in[:-offset]], axis=0
        )
        earlier = jnp.concatenate([jnp.full((offset,), -1, jnp.int32), segment[:-offset]])
        within = (earlier == segment).astype(jnp.float32)[:, None]
        convolved = convolved + kernel[KCONV - 1 - offset] * shifted * within
    activated = jax.nn.silu(convolved)
    inner = round_value(activated[:, :DI])
    in_state = round_value(activated[:, DI : DI + STATE])
    out_state = round_value(activated[:, DI + STATE :])
    step_size = jax.nn.softplus(step_raw + step_bias)
    logrates = jnp.cumsum(step_size * -jnp.exp(decay_log), axis=0)
    intersection = round_grad(jnp.dot(out_state, in_state.T, preferred_element_type=jnp.float32))
    allowed = (segment[:, None] == segment[None, :]) & (places[:, None] >= places[None, :])
    group_count = heads // 8
    rates_grouped = logrates.reshape(rows_count, group_count, 8).transpose(1, 0, 2)
    steps_grouped = step_size.reshape(rows_count, group_count, 8).transpose(1, 0, 2)
    inner_grouped = inner.reshape(rows_count, group_count, 8, HEAD).transpose(1, 0, 2, 3)

    def mix_group(entry):
        rate_part, step_part, inner_part = entry
        spread = rate_part.T[:, :, None] - rate_part.T[:, None, :]
        weights = round_value(
            intersection[None]
            * jnp.exp(jnp.where(allowed[None], spread, -1e30))
            * step_part.T[:, None, :]
        )
        return jnp.einsum("hts,shp->thp", weights, inner_part, preferred_element_type=jnp.float32)

    mixed = lax.map(jax.checkpoint(mix_group), (rates_grouped, steps_grouped, inner_grouped))
    scanned = round_grad(mixed.transpose(1, 0, 2, 3).reshape(rows_count, DI)) + inner * jnp.repeat(
        skip_gain, HEAD
    )
    gated = scanned * jax.nn.silu(gate_raw)
    gatesq = jnp.mean(gated * gated, axis=1, keepdims=True)
    normed_two = gated * lax.rsqrt(gatesq + epsilon) * gate_gain
    output = round_grad(
        jnp.dot(round_value(normed_two), weight_out, preferred_element_type=jnp.float32)
    )
    return resid + output


def adamw(weight, gradient, first, second, rate, decay):
    first_new = beta_one * first + (1.0 - beta_one) * gradient
    second_new = beta_two * second + (1.0 - beta_two) * gradient * gradient
    corrected = (
        first_new
        / (1.0 - beta_one**STEP)
        / (jnp.sqrt(second_new / (1.0 - beta_two**STEP)) + adam_eps)
    )
    master = weight.astype(jnp.float32)
    return (master - rate * (corrected + decay * master), first_new, second_new)


def reduce_group(grads):
    shares = (
        lax.psum_scatter(grads[0], "shard", scatter_dimension=0, tiled=True),
        lax.psum_scatter(grads[1], "shard", scatter_dimension=0, tiled=True),
        lax.psum_scatter(grads[2], "shard", scatter_dimension=0, tiled=True),
    )
    return lax.psum((shares[0], shares[1], shares[2]), "replica")


def on_device(
    tokens, cotangent, seq_lengths, w_in, w_out, w_small, m_in, v_in, m_out, v_out, m_small, v_small
):
    round_value, round_grad = make_rounders()
    full_in, full_out, full_small = (
        lax.all_gather(w_in, "shard", axis=0, tiled=True),
        lax.all_gather(w_out, "shard", axis=0, tiled=True),
        lax.all_gather(w_small, "shard", axis=0, tiled=True),
    )
    seglens = seq_lengths[0]

    def local(resid, weight_in, weight_out, packed):
        return mixer(resid, weight_in, weight_out, packed, seglens, round_value, round_grad)

    result, pullback = jax.vjp(
        local,
        tokens.astype(jnp.float32),
        full_in.astype(jnp.float32),
        full_out.astype(jnp.float32),
        full_small.astype(jnp.float32),
    )
    places = jnp.arange(tokens.shape[0], dtype=jnp.int32)
    valid = (places < tokens.shape[0] - seglens[-1]).astype(jnp.float32)[:, None]
    grad_x, grad_in, grad_out, grad_small = pullback(cotangent.astype(jnp.float32) * valid)
    share_in, share_out, share_small = reduce_group((grad_in, grad_out, grad_small))
    new_w_in, new_m_in, new_v_in = adamw(w_in, share_in, m_in, v_in, 0.05, 0.1)
    new_w_out, new_m_out, new_v_out = adamw(w_out, share_out, m_out, v_out, 0.04, 0.1)
    new_w_small, new_m_small, new_v_small = adamw(w_small, share_small, m_small, v_small, 0.3, 0.0)
    return (
        result.astype(jnp.bfloat16),
        grad_x.astype(jnp.bfloat16),
        new_w_in,
        new_m_in,
        new_v_in,
        new_w_out,
        new_m_out,
        new_v_out,
        new_w_small,
        new_m_small,
        new_v_small,
    )


def solution(mesh):
    in_specs = (
        P(("replica", "shard"), None),
        P(("replica", "shard"), None),
        P(("replica", "shard"), None),
        P("shard", None),
        P("shard", None),
        P("shard"),
        P("shard", None),
        P("shard", None),
        P("shard", None),
        P("shard", None),
        P("shard"),
        P("shard"),
    )
    out_specs = (
        P(("replica", "shard"), None),
        P(("replica", "shard"), None),
        P("shard", None),
        P("shard", None),
        P("shard", None),
        P("shard", None),
        P("shard", None),
        P("shard", None),
        P("shard"),
        P("shard"),
        P("shard"),
    )
    return jax.shard_map(
        on_device, mesh=mesh, in_specs=in_specs, out_specs=out_specs, check_vma=False
    )
```

profile of v0, /device:TPU:0, one launch (start us, length us, event | category | flops | bytes accessed | tf_op | source)
XLA Modules:
  0.0 397.5 jit_solution(6767632632274704854)
XLA Ops:
  11.7 13.3 %all-reduce.25 = bf16[11336]{0:T(1024)(128)(2,1)S(1)} all-reduce(bf16[11336]{0:T(1024)(128)(2,1)S(1)} %dynamic-update-slice), channel_id=1, replica_groups=mesh['replica'=8,'shard'=4] {'shard'}, use_global_device_ids=true, to_apply=%add.25 | all-reduce | flops 11336 | bytes 45344
  30.4 22.9 %all-gather.3.cloned.1.call-done = bf16[768,3352]{1,0:T(8,128)(2,1)} async-done(((bf16[192,3352]{1,0:T(8,128)(2,1)}), bf16[768,3352]{1,0:T(8,128)(2,1)}) %all-gather.3.cloned.1.call-update) | async-done | bytes 5148688 | tf_op jit(solution)/shard_map/all_gather | solution.py:141
  53.2 4.7 %fusion.63 = f32[128,3352]{0,1:T(8,128)S(1)} fusion(bf16[128,768]{1,0:T(8,128)(2,1)S(1)} %fusion.30, bf16[768,3352]{1,0:T(8,128)(2,1)} %all-gather.3.cloned.1.call-done), kind=kOutput, calls=%fused_computation.140 | convolution fusion | flops 659030016 | bytes 7061504 | tf_op jit(solution)/shard_map/jvp()/dot_general | solution.py:66
  58.2 3.1 multiply_convert_fusion.2
  67.9 5.8 %while.33 = (s32[]{:T(128)}, f32[3,128,8,64]{1,3,2,0:T(8,128)}, bf16[3,128,8,64]{1,3,2,0:T(8,128)(2,1)S(1)}, f32[1,128,128]{2,1,0:T(8,128)S(1)}, f32[3,128,8]{1,...) while((s32[]{:T(128)}, f32[3,128,8,64]{1,3,2,0:T(8,128)}, ...), condition=%wide.region_5.6_spmd.clone, body=%wide.region_4.5_spmd.clone.sunk | while | flops 17432576 | bytes 1025121 | solution.py:102
  73.7 2.4 multiply_reduce_fusion.9
  76.1 2.9 all-gather.5.cloned.1.call-done
  79.0 3.4 multiply_reduce_fusion.7
  82.4 2.6 multiply_reduce_fusion.6
  86.7 2.9 fusion.67
  92.0 26.7 %while.34 = (s32[]{:T(128)}, f32[128,128]{1,0:T(8,128)}, f32[3,128,8]{1,2,0:T(8,128)}, f32[3,128,8]{1,2,0:T(8,128)}, f32[3,128,8,64]{1,3,2,0:T(8,128)}, /*index=...) while((s32[]{:T(128)}, f32[128,128]{1,0:T(8,128)}, ...), condition=%wide.region_13.14_spmd.clone, body=%wide.region_8.13_spmd.clone.sunk | while | flops 35585028 | bytes 2122423 | solution.py:102
  94.3 1.9 fusion.107
  102.7 1.9 fusion.107
  111.8 1.9 fusion.107
  121.7 2.6 reduce_window_sum.33
  136.8 5.6 %fusion.66 = f32[768,3352]{1,0:T(8,128)} fusion(bf16[128,768]{1,0:T(8,128)(2,1)S(1)} %copy-done.16, bf16[128,3352]{0,1:T(8,128)(2,1)S(1)} %add_convert_fusion), kind=kOutput, calls=%fused_computation.143 | convolution fusion | flops 659030016 | bytes 11352064 | tf_op jit(solution)/shard_map/transpose(jvp())/dot_general | solution.py:66
  142.6 86.2 %reduce-scatter.3.cloned.1.call-done = f32[192,3352]{1,0:T(8,128)} async-done(((f32[768,3352]{1,0:T(8,128)}), f32[192,3352]{1,0:T(8,128)}) %reduce-scatter.3.cloned.1.call-update) | async-done | bytes 2574352 | tf_op jit(solution)/shard_map/reduce_scatter | solution.py:129
  230.6 4.3 %fusion.31 = (f32[768]{0:T(1024)S(1)}, f32[128]{0:T(128)S(1)}, f32[128,768]{1,0:T(8,128)S(1)}) fusion(bf16[128,768]{1,0:T(8,128)(2,1)S(1)} %copy-done.9, f32[128]{0:T(128)S(1)} %copy-done.43, f32[768]{0:T(1024)S(1)} %copy-done.34, bf16[128,3352]{0,1:T(8,128)(2,1)S(1)} %add_convert_fusion, bf16[768,3352]{1,0:T(8,128)(2,1)} %all-gather.3.cloned.1.call-done), kind=kOutput, calls=%fused_computation.88 | convolution fusion | flops 659717248 | bytes 6603776 | tf_op jit(solution)/shard_map/transpose(jvp())/dot_general | solution.py:66
  235.0 11.1 %all-reduce.26 = f32[11336]{0:T(1024)S(1)} all-reduce(f32[11336]{0:T(1024)S(1)} %pad_add_fusion), channel_id=4, replica_groups=mesh['replica'=8,'shard'=4] {'shard'}, use_global_device_ids=true, to_apply=%region_31.32.clone | all-reduce | flops 11336 | bytes 90688
  246.2 39.6 %psum.23 = f32[2834]{0:T(1024)S(1)} all-reduce(f32[2834]{0:T(1024)S(1)} %dynamic-slice.2), channel_id=1, replica_groups=mesh['replica'=8,'shard'=4] {'replica'}, use_global_device_ids=true, to_apply=%region_32.33 | all-reduce | flops 2834 | bytes 22672 | tf_op jit(solution)/shard_map/psum | solution.py:133
  287.3 2.9 fusion.22
  290.2 90.3 %all-reduce.30.cloned.1.call-done = (f32[192,3352]{1,0:T(8,128)}, f32[384,768]{1,0:T(8,128)}) async-done(((f32[192,3352]{1,0:T(8,128)}, f32[384,768]{1,0:T(8,128)}), (f32[192,3352]{1,0:T(8,128)}, f32[384,768]{1,0:T(8,128)})) %all-reduce.30.cloned.1.call-update) | async-done | bytes 3754000 | tf_op jit(solution)/shard_map/psum | solution.py:133
  380.5 8.0 %convert_subtract_fusion = (f32[192,3352]{1,0:T(8,128)}, f32[192,3352]{1,0:T(8,128)}, f32[192,3352]{1,0:T(8,128)}) fusion(bf16[192,3352]{1,0:T(8,128)(2,1)S(1)} %copy-done.7, f32[192,3352]{1,0:T(8,128)} %get-tuple-element.467, f32[192,3352]{1,0:T(8,128)} %param.22, f32[192,3352]{1,0:T(8,128)} %param.23), kind=kLoop, calls=%fused_computation.33 | loop fusion | flops 10297344 | bytes 16733184 | tf_op jit(solution)/shard_map/sub | solution.py:124
  388.6 2.4 convert_subtract_fusion.1
  (223 shorter events, 64.2 us)
Async XLA Ops:
  7.2 46.0 %all-gather.3.cloned.1.call-start = ((), (), s32[]{:S(2)}) async-start(), calls=%async_computation.2 | async-start | bytes 6635520 | tf_op jit(solution)/shard_map/all_gather | solution.py:141
  7.9 71.0 %all-gather.5.cloned.1.call-start = ((), (), s32[]{:S(2)}) async-start(), calls=%async_computation.3 | async-start | bytes 2949120 | tf_op jit(solution)/shard_map/all_gather | solution.py:142
  8.7 133.9 %reduce-scatter.5.cloned.1.call-start = ((), (), s32[]{:S(2)}) async-start(), calls=%async_computation.5 | async-start | bytes 5898240 | tf_op jit(solution)/shard_map/reduce_scatter | solution.py:130
  25.0 33.1 %copy-start.24 = (f32[1792]{0:T(1024)}, f32[1792]{0:T(1024)S(1)}, u32[]{:S(2)}) copy-start(f32[1792]{0:T(1024)S(1)} %get-tuple-element.513) | copy-start | bytes 21508
  25.1 33.1 %copy-start.26 = (f32[1792]{0:T(1024)}, f32[1792]{0:T(1024)S(1)}, u32[]{:S(2)}) copy-start(f32[1792]{0:T(1024)S(1)} %get-tuple-element.516) | copy-start | bytes 21508
  28.8 33.1 %copy-start.44 = (f32[24]{0:T(128)}, f32[24]{0:T(128)S(1)}, u32[]{:S(2)}) copy-start(f32[24]{0:T(128)S(1)} %get-tuple-element.510) | copy-start | bytes 292
  28.8 33.1 %copy-start.45 = (f32[24]{0:T(128)}, f32[24]{0:T(128)S(1)}, u32[]{:S(2)}) copy-start(f32[24]{0:T(128)S(1)} %get-tuple-element.524) | copy-start | bytes 292
  29.0 53.4 %copy-start.23 = (f32[1536]{0:T(1024)}, f32[1536]{0:T(1024)S(1)}, u32[]{:S(2)}) copy-start(f32[1536]{0:T(1024)S(1)} %mul.556) | copy-start | bytes 18436
  89.6 139.2 %reduce-scatter.3.cloned.1.call-start = ((), (), s32[]{:S(2)}) async-start(), calls=%async_computation.4 | async-start | bytes 13271040 | tf_op jit(solution)/shard_map/reduce_scatter | solution.py:129
  142.4 87.0 %copy-start.38 = (f32[1792]{0:T(1024)S(1)}, f32[1792]{0:T(1024)}, u32[]{:S(2)}) copy-start(f32[1792]{0:T(1024)} %get-tuple-element.476) | copy-start | bytes 21508
  142.4 87.1 %copy-start.37 = (f32[1536]{0:T(1024)S(1)}, f32[1536]{0:T(1024)}, u32[]{:S(2)}) copy-start(f32[1536]{0:T(1024)} %get-tuple-element.472) | copy-start | bytes 18436
  142.4 87.3 %copy-start.57 = (f32[24]{0:T(128)S(1)}, f32[24]{0:T(128)}, u32[]{:S(2)}) copy-start(f32[24]{0:T(128)} %get-tuple-element.501) | copy-start | bytes 292
  142.5 88.0 %copy-start.9 = (bf16[128,768]{1,0:T(8,128)(2,1)S(1)}, bf16[128,768]{1,0:T(8,128)(2,1)}, u32[]{:S(2)}) copy-start(bf16[128,768]{1,0:T(8,128)(2,1)} %param.16) | copy-start | bytes 589828
  142.5 88.0 %copy-start.34 = (f32[768]{0:T(1024)S(1)}, f32[768]{0:T(1024)}, u32[]{:S(2)}) copy-start(f32[768]{0:T(1024)} %copy-done.33) | copy-start | bytes 9220
  142.5 88.0 %copy-start.43 = (f32[128]{0:T(128)S(1)}, f32[128]{0:T(128)}, u32[]{:S(2)}) copy-start(f32[128]{0:T(128)} %copy-done.42) | copy-start | bytes 1540
  142.5 238.0 %all-reduce.30.cloned.1.call-start = ((), (), s32[]{:S(2)}) async-start(), calls=%async_computation.6 | async-start | bytes 7667712 | tf_op jit(solution)/shard_map/psum | solution.py:133
  230.5 55.3 %copy-start.56 = (f32[128]{0:T(128)S(1)}, f32[128]{0:T(128)}, u32[]{:S(2)}) copy-start(f32[128]{0:T(128)} %copy-done.55) | copy-start | bytes 1540
  230.5 55.3 %copy-start.39 = (bf16[2834]{0:T(1024)(128)(2,1)S(1)}, bf16[2834]{0:T(1024)(128)(2,1)}, u32[]{:S(2)}) copy-start(bf16[2834]{0:T(1024)(128)(2,1)} %param.21) | copy-start | bytes 17008
  230.5 55.3 %copy-start.40 = (f32[2834]{0:T(1024)S(1)}, f32[2834]{0:T(1024)}, u32[]{:S(2)}) copy-start(f32[2834]{0:T(1024)} %param.26) | copy-start | bytes 34012
  230.5 55.3 %copy-start.41 = (f32[2834]{0:T(1024)S(1)}, f32[2834]{0:T(1024)}, u32[]{:S(2)}) copy-start(f32[2834]{0:T(1024)} %param.27) | copy-start | bytes 34012
  230.5 55.9 %copy-start.21 = (bf16[128,768]{1,0:T(8,128)(2,1)S(1)}, bf16[128,768]{1,0:T(8,128)(2,1)}, u32[]{:S(2)}) copy-start(bf16[128,768]{1,0:T(8,128)(2,1)} %param.17) | copy-start | bytes 589828
  230.6 55.9 %copy-start.53 = (f32[128]{0:T(128)S(1)}, f32[128]{0:T(128)}, u32[]{:S(2)}) copy-start(f32[128]{0:T(128)} %copy-done.52) | copy-start | bytes 1540
  230.6 56.8 %copy-start.12 = (bf16[128,1536]{0,1:T(8,128)(2,1)S(1)}, bf16[128,1536]{0,1:T(8,128)(2,1)}, u32[]{:S(2)}) copy-start(bf16[128,1536]{0,1:T(8,128)(2,1)} %copy-done.11) | copy-start | bytes 1179652
  234.9 145.6 %copy-start.7 = (bf16[192,3352]{1,0:T(8,128)(2,1)S(1)}, bf16[192,3352]{1,0:T(8,128)(2,1)}, u32[]{:S(2)}) copy-start(bf16[192,3352]{1,0:T(8,128)(2,1)} %param.19) | copy-start | bytes 3861508
  (39 other events, 427.8 us)
Sparse Core Ops, SparseCore 0:
  9.6 43.5 all-gather.2
  54.8 24.1 all-gather.4
  89.7 47.8 reduce-scatter.4
  142.5 86.1 reduce-scatter.2
  232.7 147.7 all-reduce.29
where the time goes:
time: 399 us; the launch traced here: 397 us
  waiting for transfers between devices  204 us (51%)
  blocking collectives  64 us (16%)
  other arithmetic  47.1 us (12%)
  matrix products  38 us (10%)
  local copies, waits for them, and re-layouts  27.8 us (7%)
  between operations  16.5 us (4%)
    psum x1, waiting for transfers between devices, reduce_group(): return lax.psum((shares[0], shares[1], shares[2]), 'replica')  90.3 us
    reduce_scatter x1, waiting for transfers between devices, reduce_group(): lax.psum_scatter(grads[0], 'shard', scatter_dimension=0, tiled=True)  86.2 us
    psum x1, blocking collectives, reduce_group(): return lax.psum((shares[0], shares[1], shares[2]), 'replica')  39.6 us
    unnamed x2, blocking collectives  24.3 us
    all_gather x1, waiting for transfers between devices, on_device(): lax.all_gather(w_in, 'shard', axis=0, tiled=True)  22.9 us
    dot_general x3, matrix products, mixer(): jnp.dot(round_value(normed), weight_in, preferred_element_type=jnp.float32)  14.6 us
    dot_general x9, matrix products, mix_group(): jnp.einsum('hts,shp->thp', weights, inner_part, preferred_element_type=jn...  11.5 us
    sub x3, other arithmetic, adamw(): return (master - rate * (corrected + decay * master), first_new, second_new)  11 us
  transfers between devices with their start and end apart: 5, of which 4 were waited for; matrix products, arithmetic and copies ran while one was open for 23% of the time, Pallas kernels for 0%

commit v1 on v0

--- a/solution.py
+++ b/solution.py
@@ -1,6 +1,8 @@
 import jax
 import jax.numpy as jnp
 from jax import lax
+from jax.experimental import pallas as pl
+from jax.experimental.pallas import tpu as pltpu
 from jax.sharding import PartitionSpec as P
 
 D = 768
@@ -176,6 +178,530 @@
     )
 
 
+CHAN = DI + 2 * STATE
+HEADS = DI // HEAD
+CIN = DI + CHAN + HEADS
+MAIN = DI + CHAN
+PADC = MAIN + 128
+T = 128
+PIECES = 4
+PR = 48
+CH = 8
+CW = 640
+SROWS = 24
+MESH = pl.DeviceIdType.MESH
+VMEM_BYTES = 58 * 1024 * 1024
+BF = jnp.bfloat16
+F32 = jnp.float32
+
+
+def place():
+    replica, shard = lax.axis_index("replica"), lax.axis_index("shard")
+    return replica // 2, replica % 2, shard // 2, shard % 2
+
+
+def target(z, x, y, c):
+    return (z * 2 + x, y * 2 + c)
+
+
+def greet(peers):
+    barrier = pltpu.get_barrier_semaphore()
+    for peer in peers:
+        pl.semaphore_signal(barrier, inc=1, device_id=peer, device_id_type=MESH)
+    pl.semaphore_wait(barrier, len(peers))
+
+
+def send(src, dst, send_sem, recv_sem, peer):
+    copy = pltpu.make_async_remote_copy(
+        src_ref=src, dst_ref=dst, send_sem=send_sem, recv_sem=recv_sem,
+        device_id=peer, device_id_type=MESH,
+    )
+    copy.start()
+    return copy
+
+
+def gather_kernel(wi, wo, sm, fi, fo, fs, loc, s_own, r_own, s_y, r_y, s_x, r_x, s_fy, r_fy, s_fx, r_fx):
+    z, x, y, c = place()
+    core, other_y, other_x = target(z, x, y, 1 - c), target(z, x, 1 - y, c), target(z, 1 - x, y, c)
+    greet((core, other_y, other_x))
+    me, far = 2 * y + c, 2 * (1 - y) + c
+    units = ((wi, fi, 96, 0, 48), (wi, fi, 96, 48, 48), (wo, fo, 192, 0, 96), (wo, fo, 192, 96, 96))
+    over_y = []
+    for u, (src, full, half, first, rows) in enumerate(units):
+        here = pl.ds(pl.multiple_of(x * half + first, 16), rows)
+        over_y.append(send(src.at[here], full.at[me, here], s_y.at[u], r_y.at[u], other_y))
+    over_y.append(send(sm, fs.at[me], s_y.at[4], r_y.at[4], other_y))
+    own = [
+        send(src, full.at[me], s_own.at[i], r_own.at[i], core)
+        for i, (src, full) in enumerate(((wi, fi), (wo, fo), (sm, fs)))
+    ]
+    keep = [
+        pltpu.make_async_copy(src, full.at[me], loc.at[i])
+        for i, (src, full) in enumerate(((wi, fi), (wo, fo), (sm, fs)))
+    ]
+    for copy in keep:
+        copy.start()
+    over_x, on_y, on_x = [], [], []
+    for u, (src, full, half, first, rows) in enumerate(units):
+        here = pl.ds(pl.multiple_of(x * half + first, 16), rows)
+        over_y[u].wait_recv()
+        part = full.at[far, here]
+        over_x.append(send(part, part, s_x.at[u], r_x.at[u], other_x))
+        on_y.append(send(part, part, s_fy.at[u], r_fy.at[u], core))
+    over_y[4].wait_recv()
+    on_y.append(send(fs.at[far], fs.at[far], s_fy.at[4], r_fy.at[4], core))
+    for u, (src, full, half, first, rows) in enumerate(units):
+        there = pl.ds(pl.multiple_of((1 - x) * half + first, 16), rows)
+        over_x[u].wait_recv()
+        part = full.at[far, there]
+        on_x.append(send(part, part, s_fx.at[u], r_fx.at[u], core))
+    for copy in keep:
+        copy.wait()
+    for copy in own + on_y + on_x:
+        copy.wait_recv()
+    for copy in over_y + own + over_x + on_y + on_x:
+        copy.wait_send()
+
+
+def gather_weights(w_in, w_out, small):
+    dma = pltpu.SemaphoreType.DMA
+    return pl.pallas_call(
+        gather_kernel,
+        out_shape=(
+            jax.ShapeDtypeStruct((4, 192, CIN), BF),
+            jax.ShapeDtypeStruct((4, 384, D), BF),
+            jax.ShapeDtypeStruct((4, 32, 128), BF),
+        ),
+        in_specs=[pl.BlockSpec(memory_space=pl.ANY)] * 3,
+        out_specs=[pl.BlockSpec(memory_space=pl.ANY)] * 3,
+        scratch_shapes=[dma((3,)), dma((3,)), dma((3,)), dma((5,)), dma((5,)), dma((4,)), dma((4,)),
+                        dma((5,)), dma((5,)), dma((4,)), dma((4,))],
+        compiler_params=pltpu.CompilerParams(collective_id=0, has_side_effects=True),
+        name="gather_weights",
+    )(w_in, w_out, small)
+
+
+def dot(a, b):
+    return jnp.dot(a, b, preferred_element_type=F32)
+
+
+def dot_nt(a, b):
+    return lax.dot_general(a, b, (((1,), (1,)), ((), ())), preferred_element_type=F32)
+
+
+def dot_tn(a, b):
+    return lax.dot_general(a, b, (((0,), (0,)), ((), ())), preferred_element_type=F32)
+
+
+def colsum(v):
+    return jnp.sum(v, axis=0, keepdims=True)
+
+
+def layer_kernel(
+    x_ref, ct_ref, len_ref, wi_ref, wo_ref, taps_ref, cb_ref, head_ref, skip_ref, pg_ref, gg_ref,
+    out_ref, gx_ref, g_ref, gtaps_ref, gcb_ref, ghead_ref, gskip_ref, gpg_ref, ggg_ref,
+    gate, ci, conv, inner, scan, mixes, dproj, tail, nt, n2t, gated, n16, dn2_keep, dact,
+):
+    bounds = [len_ref[0, 0]]
+    for i in range(1, 4):
+        bounds.append(bounds[-1] + len_ref[0, i])
+    row = lax.broadcasted_iota(jnp.int32, (T, 1), 0)
+    lane = lax.broadcasted_iota(jnp.int32, (1, T), 1)
+
+    def segment(places):
+        total = jnp.zeros(places.shape, jnp.int32)
+        for bound in bounds:
+            total = total + (places >= bound).astype(jnp.int32)
+        return total
+
+    seg_row, seg_lane = segment(row), segment(lane)
+    within = [None] + [
+        ((row >= j) & (segment(row - j) == seg_row)).astype(F32) for j in range(1, KCONV)
+    ]
+    allowed = (seg_row == seg_lane) & (row >= lane)
+    valid = (row < bounds[2]).astype(F32)
+
+    x = x_ref[...].astype(F32)
+    r1 = lax.rsqrt(jnp.mean(x * x, axis=1, keepdims=True) + epsilon)
+    normed = x * r1 * pg_ref[...]
+    n16[...] = normed.astype(BF)
+    nt[...] = normed.T.astype(BF)
+    tail[...] = jnp.zeros(tail.shape, BF)
+    tail[:, :HEADS] = wi_ref[:, MAIN:]
+    n = n16[...]
+    step_in = dot(n, tail[...]) + head_ref[0:1, :]
+    for k in range(0, DI, 512):
+        gate[:, k:k + 512] = dot(n, wi_ref[:, k:k + 512])
+    W = 256
+    for k in range(0, CHAN, W):
+        cols = slice(k, k + W)
+        v = dot(n, wi_ref[:, DI + k:DI + k + W])
+        ci[:, cols] = v
+        total = cb_ref[:, cols] + taps_ref[KCONV - 1:KCONV, cols] * v
+        for j in range(1, KCONV):
+            total = total + taps_ref[KCONV - 1 - j:KCONV - j, cols] * pltpu.roll(v, j, 0) * within[j]
+        conv[:, cols] = total
+        inner[:, cols] = (total * jax.nn.sigmoid(total)).astype(BF)
+    step = jnp.maximum(step_in, 0.0) + jnp.log1p(jnp.exp(-jnp.abs(step_in)))
+    rate = -jnp.exp(head_ref[1:2, :])
+    tri = (row >= lane).astype(F32)
+    logs = jnp.dot(tri, step * rate, precision=lax.Precision.HIGHEST, preferred_element_type=F32)
+    logs_t, step_t = logs.T, step.T
+    in_state, out_state = inner[:, DI:DI + STATE], inner[:, DI + STATE:]
+    inter = dot_nt(out_state, in_state)
+    left = lane < HEAD
+    gsq = jnp.zeros((T, 1), F32)
+    for q in range(HEADS // 2):
+        cols = slice(128 * q, 128 * q + 128)
+        pair = inner[:, cols]
+        parts = []
+        for h in (2 * q, 2 * q + 1):
+            spread = logs[:, h:h + 1] - logs_t[h:h + 1, :]
+            decay = jnp.exp(jnp.where(allowed, spread, -1e30))
+            mixes[h] = decay
+            parts.append(dot((inter * decay * step_t[h:h + 1, :]).astype(BF), pair))
+        value = jnp.where(left, parts[0], parts[1]) + pair.astype(F32) * skip_ref[:, cols]
+        scan[:, cols] = value
+        g = gate[:, cols]
+        value = value * (g * jax.nn.sigmoid(g))
+        gated[:, cols] = value
+        gsq = gsq + jnp.sum(value * value, axis=1, keepdims=True)
+    r2 = lax.rsqrt(gsq * (1.0 / DI) + epsilon)
+
+    dy = ct_ref[...].astype(F32) * valid
+    d16 = dy.astype(BF)
+    out = x
+    mean_ug = jnp.zeros((T, 1), F32)
+    for k in range(0, DI, W):
+        cols = slice(k, k + W)
+        g = gated[:, cols]
+        two = g * r2 * gg_ref[:, cols]
+        two16 = two.astype(BF)
+        n2t[cols, :] = two.T.astype(BF)
+        out = out + dot(two16, wo_ref[cols, :])
+        dn2 = dot_nt(d16, wo_ref[cols, :])
+        ggg_ref[:, cols] = colsum(dn2 * (g * r2))
+        mean_ug = mean_ug + jnp.sum(dn2 * gg_ref[:, cols] * g, axis=1, keepdims=True)
+        dn2_keep[:, cols] = dn2
+    out_ref[...] = out.astype(BF)
+    back = mean_ug * (1.0 / DI) * r2 * r2
+
+    dinter = jnp.zeros((T, T), F32)
+    dlog = jnp.zeros((T, T), F32)
+    dstep_rows, dlog_rows = [], []
+    for q in range(HEADS // 2):
+        cols = slice(128 * q, 128 * q + 128)
+        g, value, gt = gate[:, cols], scan[:, cols], gated[:, cols]
+        dgated = r2 * (dn2_keep[:, cols] * gg_ref[:, cols] - gt * back)
+        sig = jax.nn.sigmoid(g)
+        dscan = dgated * (g * sig)
+        dproj[:, cols] = (dgated * value * (sig * (1.0 + g * (1.0 - sig)))).astype(BF)
+        pair = inner[:, cols]
+        pair32 = pair.astype(F32)
+        gskip_ref[:, cols] = colsum(dscan * pair32)
+        ds16 = dscan.astype(BF)
+        parts = []
+        for side, h in enumerate((2 * q, 2 * q + 1)):
+            decay, srow = mixes[h], step_t[h:h + 1, :]
+            mine = jnp.where(left if side == 0 else jnp.logical_not(left), pair32, 0.0).astype(BF)
+            dmix = dot_nt(ds16, mine) * decay
+            dinter = dinter + dmix * srow
+            wide = dmix * inter
+            per_source = colsum(wide)
+            dstep_rows.append(per_source)
+            dlog_rows.append(-per_source * srow)
+            dlog = dlog + jnp.where(lane == h, jnp.sum(wide * srow, axis=1, keepdims=True), 0.0)
+            parts.append(dot_tn((inter * decay * srow).astype(BF), ds16))
+        dact[:, cols] = jnp.where(left, parts[0], parts[1]) + dscan * skip_ref[:, cols]
+    rest = jnp.zeros((T - HEADS, T), F32)
+    dstep = jnp.concatenate(dstep_rows + [rest], axis=0).T
+    dlog = dlog + jnp.concatenate(dlog_rows + [rest], axis=0).T
+    di16 = dinter.astype(BF)
+    dact[:, DI:DI + STATE] = dot_tn(di16, out_state)
+    dact[:, DI + STATE:] = dot(di16, in_state)
+    upper = (row <= lane).astype(F32)
+    ddecay = jnp.dot(upper, dlog, precision=lax.Precision.HIGHEST, preferred_element_type=F32)
+    dstep = dstep + ddecay * rate
+    draw = dstep * jax.nn.sigmoid(step_in)
+    ghead_ref[0:1, :] = colsum(draw)
+    ghead_ref[1:2, :] = colsum(ddecay * step * rate)
+    dproj[:, MAIN:] = draw.astype(BF)
+    for k in range(0, CHAN, W):
+        cols = slice(k, k + W)
+        v, raw = conv[:, cols], ci[:, cols]
+        sig = jax.nn.sigmoid(v)
+        dconv = dact[:, cols] * (sig * (1.0 + v * (1.0 - sig)))
+        gcb_ref[:, cols] = colsum(dconv)
+        gtaps_ref[KCONV - 1:KCONV, cols] = colsum(dconv * raw)
+        dci = dconv * taps_ref[KCONV - 1:KCONV, cols]
+        for j in range(1, KCONV):
+            here = dconv * within[j]
+            gtaps_ref[KCONV - 1 - j:KCONV - j, cols] = colsum(here * pltpu.roll(raw, j, 0))
+            dci = dci + pltpu.roll(here * taps_ref[KCONV - 1 - j:KCONV - j, cols], T - j, 0)
+        dproj[:, DI + k:DI + k + W] = dci.astype(BF)
+
+    dn = dot_nt(dproj[:, MAIN:], tail[...])
+    for k in range(0, MAIN, 256):
+        dn = dn + dot_nt(dproj[:, k:k + 256], wi_ref[:, k:k + 256])
+    xr = x * r1
+    gpg_ref[...] = colsum(dn * xr)
+    u = dn * pg_ref[...]
+    dx = r1 * (u - xr * jnp.mean(u * xr, axis=1, keepdims=True)) + dy
+    gx_ref[...] = dx.astype(BF)
+
+    def put(shard, chunk, first, value):
+        wide = value.shape[1]
+        g_ref[shard, :, chunk, :, first:first + wide] = value.astype(BF).reshape(PIECES, PR, wide)
+
+    for s in range(4):
+        left_rows = nt[192 * s:192 * s + 192, :]
+        for k in range(5):
+            put(s, k, 0, dot(left_rows, dproj[:, CW * k:CW * k + CW]))
+        put(s, 5, 0, dot(left_rows, dproj[:, 5 * CW:]))
+        rows_a = n2t[384 * s:384 * s + 192, :]
+        rows_b = n2t[384 * s + 192:384 * s + 384, :]
+        put(s, 5, 256, dot(rows_a, d16[:, :384]))
+        put(s, 6, 0, dot(rows_a, d16[:, 384:]))
+        put(s, 6, 384, dot(rows_b, d16[:, :256]))
+        put(s, 7, 0, dot(rows_b, d16[:, 256:]))
+        put(s, 7, 512, jnp.zeros((192, 128), F32))
+
+
+def layer(tokens, cotangent, lens, w_in, w_out, taps, cb, head, skip, pg, gg):
+    vmem = pl.BlockSpec(memory_space=pltpu.VMEM)
+    shape = jax.ShapeDtypeStruct
+    return pl.pallas_call(
+        layer_kernel,
+        out_shape=(
+            shape((T, D), BF), shape((T, D), BF), shape((4, PIECES, CH, PR, CW), BF),
+            shape((KCONV, CHAN), F32), shape((1, CHAN), F32), shape((2, 128), F32),
+            shape((1, DI), F32), shape((1, D), F32), shape((1, DI), F32),
+        ),
+        in_specs=[vmem, vmem, pl.BlockSpec(memory_space=pltpu.SMEM)] + [vmem] * 8,
+        out_specs=[vmem] * 9,
+        scratch_shapes=[
+            pltpu.VMEM((T, DI), F32), pltpu.VMEM((T, CHAN), F32), pltpu.VMEM((T, CHAN), F32),
+            pltpu.VMEM((T, CHAN), BF), pltpu.VMEM((T, DI), F32), pltpu.VMEM((HEADS, T, T), F32),
+            pltpu.VMEM((T, PADC), BF), pltpu.VMEM((D, 128), BF), pltpu.VMEM((D, T), BF),
+            pltpu.VMEM((DI, T), BF), pltpu.VMEM((T, DI), F32), pltpu.VMEM((T, D), BF),
+            pltpu.VMEM((T, DI), F32), pltpu.VMEM((T, CHAN), F32),
+        ],
+        compiler_params=pltpu.CompilerParams(vmem_limit_bytes=VMEM_BYTES),
+        name="layer",
+    )(tokens, cotangent, lens, w_in, w_out, taps, cb, head, skip, pg, gg)
+
+
+def reduce_kernel(
+    g, sm, red, sm_out, own, rc, r1, r2, rz, sbuf, srecv,
+    loc, s_c, r_c, s_1, r_1, s_2, r_2, s_z, r_z, s_g, r_g, s_x, r_x, s_s, r_s,
+):
+    z, x, y, c = place()
+    core, other_y, other_x = target(z, x, y, 1 - c), target(z, x, 1 - y, c), target(z, 1 - x, y, c)
+    others = [lax.rem(z + d, 4) for d in (1, 2, 3)]
+    over_z = [target(o, x, y, c) for o in others]
+    greet([core, other_y, other_x] + over_z)
+    started = []
+
+    def go(*args):
+        copy = send(*args)
+        started.append(copy)
+        return copy
+
+    mine, away = pl.ds(4 * x, 4), pl.ds(4 * (1 - x), 4)
+    first = []
+    small_copy = go(sm, srecv.at[0], s_s.at[0], r_s.at[0], core)
+    for p in range(PIECES):
+        first.append([
+            go(g.at[2 * i + 1 - c, p], rc.at[i, p], s_c.at[p, i], r_c.at[p, i], core) for i in range(2)
+        ])
+    keep = [
+        [pltpu.make_async_copy(g.at[2 * i + c, p], own.at[i, p], loc.at[p, i]) for i in range(2)]
+        for p in range(PIECES)
+    ]
+    for pair in keep:
+        for copy in pair:
+            copy.start()
+
+    def add(dst, src, chunks):
+        def step(i, carry):
+            a, b = dst.at[i], src.at[i]
+            a[...] = (a[...].astype(F32) + b[...].astype(F32)).astype(BF)
+            return carry
+
+        lax.fori_loop(0, chunks, step, 0)
+
+    second = []
+    for p in range(PIECES):
+        for i in range(2):
+            keep[p][i].wait()
+            first[p][i].wait_recv()
+            add(own.at[i, p], rc.at[i, p], CH)
+        if p % 2 == 0:
+            second.append([go(own.at[1 - y, p], r1.at[p], s_1.at[p, 0], r_1.at[p, 0], other_y)])
+        else:
+            second.append([
+                go(own.at[i, p, away], r1.at[p, pl.ds(4 * i, 4)], s_1.at[p, i], r_1.at[p, i], other_x)
+                for i in range(2)
+            ])
+    small_copy.wait_recv()
+    sbuf[0] = sm[...] + srecv[0]
+    small_copy = go(sbuf.at[0], srecv.at[1], s_s.at[1], r_s.at[1], other_y)
+    third = []
+    for p in range(PIECES):
+        for copy in second[p]:
+            copy.wait_recv()
+        if p % 2 == 0:
+            add(own.at[y, p], r1.at[p], CH)
+            third.append(go(own.at[y, p, away], r2.at[p], s_2.at[p], r_2.at[p], other_x))
+        else:
+            for i in range(2):
+                add(own.at[i, p, mine], r1.at[p, pl.ds(4 * i, 4)], 4)
+            third.append(go(own.at[1 - y, p, mine], r2.at[p], s_2.at[p], r_2.at[p], other_y))
+    small_copy.wait_recv()
+    sbuf[1] = sbuf[0] + srecv[1]
+    small_copy = go(sbuf.at[1], srecv.at[2], s_s.at[2], r_s.at[2], other_x)
+    spread = []
+    for p in range(PIECES):
+        third[p].wait_recv()
+        add(own.at[y, p, mine], r2.at[p], 4)
+        spread.append([
+            go(own.at[y, p, 4 * x + others[d]], rz.at[p, d], s_z.at[p, d], r_z.at[p, d], over_z[d])
+            for d in range(3)
+        ])
+    small_copy.wait_recv()
+    sbuf[2] = sbuf[1] + srecv[2]
+    small = [go(sbuf.at[2], srecv.at[3 + d], s_s.at[3 + d], r_s.at[3 + d], over_z[d]) for d in range(3)]
+    back = []
+    for p in range(PIECES):
+        for copy in spread[p]:
+            copy.wait_recv()
+        total = own[y, p, 4 * x + z].astype(F32)
+        for d in range(3):
+            total = total + rz[p, d].astype(F32)
+        at = red.at[p, 4 * x + z]
+        at[...] = total.astype(BF)
+        back.append([go(at, at, s_g.at[p, d], r_g.at[p, d], over_z[d]) for d in range(3)])
+    last = []
+    for p in range(PIECES):
+        for copy in back[p]:
+            copy.wait_recv()
+        at = red.at[p, mine]
+        last.append(go(at, at, s_x.at[p], r_x.at[p], other_x))
+    for copy in small:
+        copy.wait_recv()
+    pieces = [sbuf[2], srecv[3], srecv[4], srecv[5]]
+    here = jnp.zeros(here_shape, F32)
+    for zi in range(4):
+        back_by = lax.rem(z - zi + 4, 4)
+        pick = pieces[0]
+        for d in (1, 2, 3):
+            pick = jnp.where(back_by == d, pieces[d], pick)
+        here = here + pick
+    mine_rows = jnp.where(y == 0, jnp.where(c == 0, here[0], here[1]), jnp.where(c == 0, here[2], here[3]))
+    sm_out[...] = mine_rows
+    for copy in last:
+        copy.wait_recv()
+    for copy in started:
+        copy.wait_send()
+
+
+here_shape = (4, SROWS, 128)
+
+
+def reduce_grads(g, small):
+    dma = pltpu.SemaphoreType.DMA
+    vmem = pl.BlockSpec(memory_space=pltpu.VMEM)
+    return pl.pallas_call(
+        reduce_kernel,
+        out_shape=(
+            jax.ShapeDtypeStruct((PIECES, CH, PR, CW), BF),
+            jax.ShapeDtypeStruct((SROWS, 128), F32),
+        ),
+        in_specs=[pl.BlockSpec(memory_space=pl.ANY), vmem],
+        out_specs=[vmem, vmem],
+        scratch_shapes=[
+            pltpu.VMEM((2, PIECES, CH, PR, CW), BF), pltpu.VMEM((2, PIECES, CH, PR, CW), BF),
+            pltpu.VMEM((PIECES, CH, PR, CW), BF), pltpu.VMEM((PIECES, 4, PR, CW), BF),
+            pltpu.VMEM((PIECES, 3, PR, CW), BF),
+            pltpu.VMEM((3, 4, SROWS, 128), F32), pltpu.VMEM((6, 4, SROWS, 128), F32),
+            dma((PIECES, 2)), dma((PIECES, 2)), dma((PIECES, 2)), dma((PIECES, 2)), dma((PIECES, 2)),
+            dma((PIECES,)), dma((PIECES,)), dma((PIECES, 3)), dma((PIECES, 3)), dma((PIECES, 3)),
+            dma((PIECES, 3)), dma((PIECES,)), dma((PIECES,)), dma((6,)), dma((6,)),
+        ],
+        compiler_params=pltpu.CompilerParams(
+            collective_id=1, has_side_effects=True, vmem_limit_bytes=VMEM_BYTES
+        ),
+        name="reduce_grads",
+    )(g, small)
+
+
+def adamw_kernel(red, wi, mi, vi, wo, mo, vo, nwi, nmi, nvi, nwo, nmo, nvo):
+    def update(cols, grad, refs, rate, part=None):
+        at = (slice(None), cols) if part is None else (part, slice(None), cols)
+        new = adamw(refs[0][at], grad.astype(F32), refs[1][at], refs[2][at], rate, 0.1)
+        for ref, value in zip(refs[3:], new):
+            ref[at] = value
+
+    refs_in = (wi, mi, vi, nwi, nmi, nvi)
+    refs_out = (wo, mo, vo, nwo, nmo, nvo)
+    for k in range(5):
+        update(slice(CW * k, CW * k + CW), red[0, k], refs_in, 0.05)
+    update(slice(5 * CW, CIN), red[0, 5, :, :CIN - 5 * CW], refs_in, 0.05)
+    update(slice(0, 384), red[0, 5, :, 256:], refs_out, 0.04, 0)
+    update(slice(384, 768), red[0, 6, :, :384], refs_out, 0.04, 0)
+    update(slice(0, 256), red[0, 6, :, 384:], refs_out, 0.04, 1)
+    update(slice(256, 768), red[0, 7, :, :512], refs_out, 0.04, 1)
+
+
+def adamw_all(red, w_in, m_in, v_in, w_out, m_out, v_out):
+    rows = 16
+    halves = [v.reshape(2, 192, D) for v in (w_out, m_out, v_out)]
+    spec_in = pl.BlockSpec((rows, CIN), lambda i: (i, 0))
+    spec_out = pl.BlockSpec((2, rows, D), lambda i: (0, i, 0))
+    new = pl.pallas_call(
+        adamw_kernel,
+        grid=(192 // rows,),
+        out_shape=[jax.ShapeDtypeStruct((192, CIN), F32)] * 3 + [jax.ShapeDtypeStruct((2, 192, D), F32)] * 3,
+        in_specs=[pl.BlockSpec((1, CH, rows, CW), lambda i: (i // 3, 0, i % 3, 0))]
+        + [spec_in] * 3 + [spec_out] * 3,
+        out_specs=[spec_in] * 3 + [spec_out] * 3,
+        compiler_params=pltpu.CompilerParams(vmem_limit_bytes=VMEM_BYTES),
+        name="adamw",
+    )(red, w_in, m_in, v_in, *halves)
+    return list(new[:3]) + [v.reshape(384, D) for v in new[3:]]
+
+
+def on_device_fast(
+    tokens, cotangent, seq_lengths, w_in, w_out, w_small, m_in, v_in, m_out, v_out, m_small, v_small
+):
+    share = w_small.shape[0]
+    small = jnp.pad(w_small, (0, 32 * 128 - share)).reshape(32, 128)
+    full_in, full_out, full_small = gather_weights(w_in, w_out, small)
+    packed = full_small.reshape(4, 32 * 128)[:, :share].reshape(4 * share).astype(F32)
+    start = (KCONV + 1) * CHAN
+    taps = packed[: KCONV * CHAN].reshape(KCONV, CHAN)
+    cb = packed[KCONV * CHAN : start].reshape(1, CHAN)
+    head = jnp.pad(packed[start : start + 2 * HEADS].reshape(2, HEADS), ((0, 0), (0, 128 - HEADS)))
+    skip = jnp.repeat(packed[start + 2 * HEADS : start + 3 * HEADS], HEAD).reshape(1, DI)
+    gains = start + 3 * HEADS
+    pg = packed[gains : gains + D].reshape(1, D)
+    gg = packed[gains + D :].reshape(1, DI)
+    out, gx, g, gtaps, gcb, ghead, gskip, gpg, ggg = layer(
+        tokens, cotangent, seq_lengths, full_in.reshape(D, CIN), full_out.reshape(DI, D),
+        taps, cb, head, skip, pg, gg,
+    )
+    flat = jnp.concatenate([
+        gtaps.reshape(-1), gcb.reshape(-1), ghead[:, :HEADS].reshape(-1),
+        gskip.reshape(HEADS, HEAD).sum(axis=1), gpg.reshape(-1), ggg.reshape(-1),
+    ])
+    flat = jnp.pad(flat.reshape(4, share), ((0, 0), (0, SROWS * 128 - share))).reshape(4, SROWS, 128)
+    red, small_sum = reduce_grads(g, flat)
+    new = adamw_all(red, w_in, m_in, v_in, w_out, m_out, v_out)
+    share_small = small_sum.reshape(-1)[:share]
+    new_small = adamw(w_small, share_small, m_small, v_small, 0.3, 0.0)
+    return (out, gx, *new, *new_small)
+
+
 def solution(mesh):
     in_specs = (
         P(("replica", "shard"), None),
@@ -204,6 +730,7 @@
         P("shard"),
         P("shard"),
     )
+    fast = dict(mesh.shape) == {"replica": 8, "shard": 4}
     return jax.shard_map(
-        on_device, mesh=mesh, in_specs=in_specs, out_specs=out_specs, check_vma=False
-    )
+        on_device_fast if fast else on_device, mesh=mesh, in_specs=in_specs, out_specs=out_specs, check_vma=False
+    )

time: 399 us -> 208 us (0.52)
  waiting for transfers between devices: 204 us -> 0 us
  Pallas kernels: 0 us -> 193 us
  blocking collectives: 64 us -> 0 us
  other arithmetic: 47.1 us -> 4.3 us
  matrix products: 38 us -> 0 us
  local copies, waits for them, and re-layouts: 27.8 us -> 8.5 us
  between operations: 16.5 us -> 0.74 us
    pallas_call x0 -> x4, Pallas kernels: none -> 193 us  [the longest x1 101 us: reduce_grads(): pl.pallas_call(reduce_kernel, out_shape=(jax.ShapeDtypeStruct((PIECES, CH...]
    psum x1 -> x0, waiting for transfers between devices: 90.3 us -> none  [reduce_group(): return lax.psum((shares[0], shares[1], shares[2]), 'replica')]
    reduce_scatter x2 -> x0, waiting for transfers between devices: 86.2 us -> none  [the longest x1 86.2 us: reduce_group(): lax.psum_scatter(grads[0], 'shard', scatter_dimension=0, tiled=True)]
    psum x1 -> x0, blocking collectives: 39.6 us -> none  [reduce_group(): return lax.psum((shares[0], shares[1], shares[2]), 'replica')]
    dot_general x18 -> x0, matrix products: 38 us -> none  [the longest x3 14.6 us: mixer(): jnp.dot(round_value(normed), weight_in, preferred_element_type=jnp.float32)]
    all_gather x2 -> x0, waiting for transfers between devices: 25.7 us -> none  [the longest x1 22.9 us: on_device(): lax.all_gather(w_in, 'shard', axis=0, tiled=True)]
    unnamed x2 -> x0, blocking collectives: 24.3 us -> none
    reduce_sum x9 -> x1, other arithmetic: 10 us -> 0.12 us  [on_device_fast(): gskip.reshape(HEADS, HEAD).sum(axis=1)]
  transfers between devices with their start and end apart: 5 -> 0, of which waited for: 4 -> 0; matrix products, arithmetic and copies ran while one was open for 23% -> 0% of each run, Pallas kernels for 0% -> 0%
where the time goes in v1:
time: 208 us; the launch traced here: 207 us
  Pallas kernels  193 us (93%)
  local copies, waits for them, and re-layouts  8.5 us (4%)
  other arithmetic  4.3 us (2%)
    pallas_call x1, Pallas kernels, reduce_grads(): pl.pallas_call(reduce_kernel, out_shape=(jax.ShapeDtypeStruct((PIECES, CH...  101 us
    pallas_call x1, Pallas kernels, gather_weights(): pl.pallas_call(gather_kernel, out_shape=(jax.ShapeDtypeStruct((4, 192, CI...  62.8 us
    pallas_call x1, Pallas kernels, layer(): pl.pallas_call(layer_kernel, out_shape=(shape((T, D), BF), shape((T, D),...  16.3 us
    pallas_call x1, Pallas kernels, adamw_all(): pl.pallas_call(adamw_kernel, grid=(192 // rows,), out_shape=[jax.ShapeDty...  13.2 us

profile of v1, /device:TPU:0, one launch (start us, length us, event | category | flops | bytes accessed | tf_op | source)
XLA Modules:
  0.0 206.8 jit_solution(10286388558270233226)
XLA Ops:
  0.6 1.3 pad_bitcast_fusion.1.sm
  1.9 62.8 %gather_weights.1 = (bf16[4,192,3352]{2,1,0:T(8,128)(2,1)}, bf16[4,384,768]{2,1,0:T(8,128)(2,1)}, bf16[4,32,128]{2,1,0:T(8,128)(2,1)}) custom-call(bf16[192,3352]{1,0:T(8,128)(2,1)} %wi.3, bf16[384,768]{1,0:T(8,128)(2,1)} %wo.1, bf16[32,128]{1,0:T(8,128)(2,1)} %pad_bitcast_fusion.1.sm), custom_call_target="tpu_custom_call" | custom-call | tf_op jit(solution)/shard_map/gather_weights/pallas_call | solution.py:268
  64.8 0.8 copy.28
  65.6 0.1 reshape.121
  65.8 0.1 reshape.103
  65.8 0.5 pad.13.head_ref
  66.4 0.6 reshape.104.pg_ref
  67.1 0.6 reshape.105.gg_ref
  67.7 0.6 reshape.102.cb_ref
  68.3 0.6 reshape.101.taps_ref
  69.0 0.7 reshape_reshape.3.skip_ref
  69.7 16.3 %layer.1 = (bf16[128,768]{1,0:T(8,128)(2,1)}, bf16[128,768]{1,0:T(8,128)(2,1)}, bf16[4,4,8,48,640]{4,3,2,1,0:T(8,128)(2,1)}, f32[4,1792]{1,0:T(4,128)}, f32[1,17...) custom-call(bf16[128,768]{1,0:T(8,128)(2,1)} %x_ref.1, ...), custom_call_target="tpu_custom_call" | custom-call | tf_op jit(solution)/shard_map/layer/pallas_call | solution.py:473
  86.0 0.7 reshape.108
  86.7 0.7 reduce.2
  87.3 0.7 reduce
  88.1 0.7 reduce.1
  88.8 0.7 reduce.3
  89.6 0.1 reduce_sum.9
  89.7 0.8 reshape.106
  90.5 0.1 reshape.112
  90.7 0.6 copy.27
  91.3 100.9 %reduce_grads.1 = (bf16[4,8,48,640]{3,2,1,0:T(8,128)(2,1)}, f32[24,128]{1,0:T(8,128)}) custom-call(bf16[4,4,8,48,640]{4,3,2,1,0:T(8,128)(2,1)} %get-tuple-element.36.g, f32[4,24,128]{2,1,0:T(8,128)} %bitcast.26), custom_call_target="tpu_custom_call" | custom-call | tf_op jit(solution)/shard_map/reduce_grads/pallas_call | solution.py:614
  192.3 1.3 convert_subtract_fusion
  193.6 13.2 %adamw.1 = (f32[192,3352]{1,0:T(8,128)}, f32[192,3352]{1,0:T(8,128)}, f32[192,3352]{1,0:T(8,128)}, f32[2,192,768]{2,1,0:T(8,128)}, f32[2,192,768]{2,1,0:T(8,128)}, /*index=5*/f32[2,192,768]{2,1,0:T(8,128)}) custom-call(bf16[4,8,48,640]{3,2,1,0:T(8,128)(2,1)} %get-tuple-element.43.red, bf16[192,3352]{1,0:T(8,128)(2,1)} %wi.3, f32[192,3352]{1,0:T(8,128)} %mi.1, ...), custom_call_target="tpu_custom_call" | custom-call | tf_op jit(solution)/shard_map/adamw/pallas_call | solution.py:661
  (17 shorter events, 0.5 us)
Async XLA Ops:
  91.3 101.0 %copy-start = (bf16[2834]{0:T(1024)(128)(2,1)S(1)}, bf16[2834]{0:T(1024)(128)(2,1)}, u32[]{:S(2)}) copy-start(bf16[2834]{0:T(1024)(128)(2,1)} %param.17) | copy-start | bytes 17008
  91.3 101.0 %copy-start.1 = (f32[2834]{0:T(1024)S(1)}, f32[2834]{0:T(1024)}, u32[]{:S(2)}) copy-start(f32[2834]{0:T(1024)} %param.22) | copy-start | bytes 34012
  91.3 101.0 %copy-start.2 = (f32[2834]{0:T(1024)S(1)}, f32[2834]{0:T(1024)}, u32[]{:S(2)}) copy-start(f32[2834]{0:T(1024)} %param.23) | copy-start | bytes 34012

commit v2 on v1

--- a/solution.py
+++ b/solution.py
@@ -220,40 +220,36 @@
     return copy
 
 
-def gather_kernel(wi, wo, sm, fi, fo, fs, loc, s_own, r_own, s_y, r_y, s_x, r_x, s_fy, r_fy, s_fx, r_fx):
+def gather_kernel(wi, sm, fi, fs, loc, s_own, r_own, s_y, r_y, s_x, r_x, s_fy, r_fy, s_fx, r_fx):
     z, x, y, c = place()
     core, other_y, other_x = target(z, x, y, 1 - c), target(z, x, 1 - y, c), target(z, 1 - x, y, c)
     greet((core, other_y, other_x))
     me, far = 2 * y + c, 2 * (1 - y) + c
-    units = ((wi, fi, 96, 0, 48), (wi, fi, 96, 48, 48), (wo, fo, 192, 0, 96), (wo, fo, 192, 96, 96))
-    over_y = []
-    for u, (src, full, half, first, rows) in enumerate(units):
-        here = pl.ds(pl.multiple_of(x * half + first, 16), rows)
-        over_y.append(send(src.at[here], full.at[me, here], s_y.at[u], r_y.at[u], other_y))
-    over_y.append(send(sm, fs.at[me], s_y.at[4], r_y.at[4], other_y))
-    own = [
-        send(src, full.at[me], s_own.at[i], r_own.at[i], core)
-        for i, (src, full) in enumerate(((wi, fi), (wo, fo), (sm, fs)))
-    ]
+    over_y = [send(sm, fs.at[me], s_y.at[3], r_y.at[3], other_y)]
+    own = [send(sm, fs.at[me], s_own.at[1], r_own.at[1], core)]
+    for u in range(3):
+        here = pl.ds(pl.multiple_of(x * 96 + 32 * u, 16), 32)
+        over_y.append(send(wi.at[here], fi.at[me, here], s_y.at[u], r_y.at[u], other_y))
+    own.append(send(wi, fi.at[me], s_own.at[0], r_own.at[0], core))
     keep = [
         pltpu.make_async_copy(src, full.at[me], loc.at[i])
-        for i, (src, full) in enumerate(((wi, fi), (wo, fo), (sm, fs)))
+        for i, (src, full) in enumerate(((wi, fi), (sm, fs)))
     ]
     for copy in keep:
         copy.start()
     over_x, on_y, on_x = [], [], []
-    for u, (src, full, half, first, rows) in enumerate(units):
-        here = pl.ds(pl.multiple_of(x * half + first, 16), rows)
-        over_y[u].wait_recv()
-        part = full.at[far, here]
+    over_y[0].wait_recv()
+    on_y.append(send(fs.at[far], fs.at[far], s_fy.at[3], r_fy.at[3], core))
+    for u in range(3):
+        here = pl.ds(pl.multiple_of(x * 96 + 32 * u, 16), 32)
+        over_y[u + 1].wait_recv()
+        part = fi.at[far, here]
         over_x.append(send(part, part, s_x.at[u], r_x.at[u], other_x))
         on_y.append(send(part, part, s_fy.at[u], r_fy.at[u], core))
-    over_y[4].wait_recv()
-    on_y.append(send(fs.at[far], fs.at[far], s_fy.at[4], r_fy.at[4], core))
-    for u, (src, full, half, first, rows) in enumerate(units):
-        there = pl.ds(pl.multiple_of((1 - x) * half + first, 16), rows)
+    for u in range(3):
+        there = pl.ds(pl.multiple_of((1 - x) * 96 + 32 * u, 16), 32)
         over_x[u].wait_recv()
-        part = full.at[far, there]
+        part = fi.at[far, there]
         on_x.append(send(part, part, s_fx.at[u], r_fx.at[u], core))
     for copy in keep:
         copy.wait()
@@ -263,22 +259,21 @@
         copy.wait_send()
 
 
-def gather_weights(w_in, w_out, small):
+def gather_weights(w_in, small):
     dma = pltpu.SemaphoreType.DMA
     return pl.pallas_call(
         gather_kernel,
         out_shape=(
             jax.ShapeDtypeStruct((4, 192, CIN), BF),
-            jax.ShapeDtypeStruct((4, 384, D), BF),
             jax.ShapeDtypeStruct((4, 32, 128), BF),
         ),
-        in_specs=[pl.BlockSpec(memory_space=pl.ANY)] * 3,
-        out_specs=[pl.BlockSpec(memory_space=pl.ANY)] * 3,
-        scratch_shapes=[dma((3,)), dma((3,)), dma((3,)), dma((5,)), dma((5,)), dma((4,)), dma((4,)),
-                        dma((5,)), dma((5,)), dma((4,)), dma((4,))],
+        in_specs=[pl.BlockSpec(memory_space=pl.ANY)] * 2,
+        out_specs=[pl.BlockSpec(memory_space=pl.ANY)] * 2,
+        scratch_shapes=[dma((2,)), dma((2,)), dma((2,)), dma((4,)), dma((4,)), dma((3,)), dma((3,)),
+                        dma((4,)), dma((4,)), dma((3,)), dma((3,))],
         compiler_params=pltpu.CompilerParams(collective_id=0, has_side_effects=True),
         name="gather_weights",
-    )(w_in, w_out, small)
+    )(w_in, small)
 
 
 def dot(a, b):
@@ -298,10 +293,36 @@
 
 
 def layer_kernel(
-    x_ref, ct_ref, len_ref, wi_ref, wo_ref, taps_ref, cb_ref, head_ref, skip_ref, pg_ref, gg_ref,
-    out_ref, gx_ref, g_ref, gtaps_ref, gcb_ref, ghead_ref, gskip_ref, gpg_ref, ggg_ref,
+    x_ref, ct_ref, len_ref, wi_ref, wo_own, par_ref,
+    out_ref, gx_ref, red, sm_out,
     gate, ci, conv, inner, scan, mixes, dproj, tail, nt, n2t, gated, n16, dn2_keep, dact,
+    wo_full, d_own, d_in, n_in, n2_in, dp_in, own, half_in, rz, gs, sbuf, srecv,
+    s_w, r_w, s_d, r_d, s_n, r_n, s_2, r_2, s_p, r_p, s_h, r_h, s_z, r_z, s_g, r_g, s_x, r_x, s_s, r_s,
 ):
+    z, x_at, y, c = place()
+    core, other_y = target(z, x_at, y, 1 - c), target(z, x_at, 1 - y, c)
+    diag, other_x = target(z, x_at, 1 - y, 1 - c), target(z, 1 - x_at, y, c)
+    others = [lax.rem(z + d, 4) for d in (1, 2, 3)]
+    over_z = [target(o, x_at, y, c) for o in others]
+    greet([core, other_y, diag, other_x] + over_z)
+    started = []
+
+    def go(*args):
+        copy = send(*args)
+        started.append(copy)
+        return copy
+
+    me, far = 2 * y + c, 2 * (1 - y) + c
+    group = [(core, 2 * y + 1 - c), (other_y, far), (diag, 2 * (1 - y) + 1 - c)]
+    here = pl.ds(pl.multiple_of(x_at * 192, 16), 192)
+    there = pl.ds(pl.multiple_of((1 - x_at) * 192, 16), 192)
+    w_over_y = go(wo_own.at[here], wo_full.at[me, here], s_w.at[0], r_w.at[0], other_y)
+    w_own = go(wo_own, wo_full.at[me], s_w.at[1], r_w.at[1], core)
+    wo_full[me] = wo_own[...]
+    taps_ref, cb_ref = par_ref.at[0:4], par_ref.at[4:5]
+    pg_ref, gg_ref = par_ref.at[5:6, 0:D], par_ref.at[6:7, 0:DI]
+    step_bias, decay_log, skips = (par_ref[5:6, 768 + 128 * i:896 + 128 * i] for i in range(3))
+    gs[...] = jnp.zeros(gs.shape, F32)
     bounds = [len_ref[0, 0]]
     for i in range(1, 4):
         bounds.append(bounds[-1] + len_ref[0, i])
@@ -325,11 +346,18 @@
     r1 = lax.rsqrt(jnp.mean(x * x, axis=1, keepdims=True) + epsilon)
     normed = x * r1 * pg_ref[...]
     n16[...] = normed.astype(BF)
-    nt[...] = normed.T.astype(BF)
+    nt[...] = normed.T.astype(BF).reshape(4, 192, T)
+    dy = ct_ref[...].astype(F32) * valid
+    d16 = dy.astype(BF)
+    d_own[...] = d16
+    d_got, n_got, n2_got = [], [], []
+    for i, (peer, shard) in enumerate(group):
+        n_got.append(go(nt.at[shard], n_in.at[i], s_n.at[i], r_n.at[i], peer))
+        d_got.append(go(d_own, d_in.at[i], s_d.at[i], r_d.at[i], peer))
     tail[...] = jnp.zeros(tail.shape, BF)
     tail[:, :HEADS] = wi_ref[:, MAIN:]
     n = n16[...]
-    step_in = dot(n, tail[...]) + head_ref[0:1, :]
+    step_in = dot(n, tail[...]) + step_bias
     for k in range(0, DI, 512):
         gate[:, k:k + 512] = dot(n, wi_ref[:, k:k + 512])
     W = 256
@@ -342,14 +370,22 @@
             total = total + taps_ref[KCONV - 1 - j:KCONV - j, cols] * pltpu.roll(v, j, 0) * within[j]
         conv[:, cols] = total
         inner[:, cols] = (total * jax.nn.sigmoid(total)).astype(BF)
+    w_over_y.wait_recv()
+    part = wo_full.at[far, here]
+    w_over_x = go(part, part, s_w.at[2], r_w.at[2], other_x)
+    w_fwd = go(part, part, s_w.at[3], r_w.at[3], core)
     step = jnp.maximum(step_in, 0.0) + jnp.log1p(jnp.exp(-jnp.abs(step_in)))
-    rate = -jnp.exp(head_ref[1:2, :])
+    rate = -jnp.exp(decay_log)
     tri = (row >= lane).astype(F32)
     logs = jnp.dot(tri, step * rate, precision=lax.Precision.HIGHEST, preferred_element_type=F32)
     logs_t, step_t = logs.T, step.T
     in_state, out_state = inner[:, DI:DI + STATE], inner[:, DI + STATE:]
     inter = dot_nt(out_state, in_state)
     left = lane < HEAD
+
+    def skip_of(q):
+        return jnp.where(left, skips[:, 2 * q:2 * q + 1], skips[:, 2 * q + 1:2 * q + 2])
+
     gsq = jnp.zeros((T, 1), F32)
     for q in range(HEADS // 2):
         cols = slice(128 * q, 128 * q + 128)
@@ -360,7 +396,7 @@
             decay = jnp.exp(jnp.where(allowed, spread, -1e30))
             mixes[h] = decay
             parts.append(dot((inter * decay * step_t[h:h + 1, :]).astype(BF), pair))
-        value = jnp.where(left, parts[0], parts[1]) + pair.astype(F32) * skip_ref[:, cols]
+        value = jnp.where(left, parts[0], parts[1]) + pair.astype(F32) * skip_of(q)
         scan[:, cols] = value
         g = gate[:, cols]
         value = value * (g * jax.nn.sigmoid(g))
@@ -368,26 +404,34 @@
         gsq = gsq + jnp.sum(value * value, axis=1, keepdims=True)
     r2 = lax.rsqrt(gsq * (1.0 / DI) + epsilon)
 
-    dy = ct_ref[...].astype(F32) * valid
-    d16 = dy.astype(BF)
+    w_over_x.wait_recv()
+    part = wo_full.at[far, there]
+    w_last = go(part, part, s_w.at[4], r_w.at[4], core)
+    for copy in (w_own, w_fwd, w_last):
+        copy.wait_recv()
     out = x
     mean_ug = jnp.zeros((T, 1), F32)
+    W = 128
     for k in range(0, DI, W):
         cols = slice(k, k + W)
         g = gated[:, cols]
         two = g * r2 * gg_ref[:, cols]
         two16 = two.astype(BF)
-        n2t[cols, :] = two.T.astype(BF)
-        out = out + dot(two16, wo_ref[cols, :])
-        dn2 = dot_nt(d16, wo_ref[cols, :])
-        ggg_ref[:, cols] = colsum(dn2 * (g * r2))
+        w_part = wo_full[k // 384, k % 384:k % 384 + W, :]
+        n2t[k // 384, k % 384:k % 384 + W, :] = two.T.astype(BF)
+        out = out + dot(two16, w_part)
+        dn2 = dot_nt(d16, w_part)
+        gs[6:7, cols] = colsum(dn2 * (g * r2))
         mean_ug = mean_ug + jnp.sum(dn2 * gg_ref[:, cols] * g, axis=1, keepdims=True)
         dn2_keep[:, cols] = dn2
     out_ref[...] = out.astype(BF)
+    for i, (peer, shard) in enumerate(group):
+        n2_got.append(go(n2t.at[shard], n2_in.at[i], s_2.at[i], r_2.at[i], peer))
     back = mean_ug * (1.0 / DI) * r2 * r2
 
     dinter = jnp.zeros((T, T), F32)
     dlog = jnp.zeros((T, T), F32)
+    dskip = jnp.zeros((1, T), F32)
     dstep_rows, dlog_rows = [], []
     for q in range(HEADS // 2):
         cols = slice(128 * q, 128 * q + 128)
@@ -398,13 +442,15 @@
         dproj[:, cols] = (dgated * value * (sig * (1.0 + g * (1.0 - sig)))).astype(BF)
         pair = inner[:, cols]
         pair32 = pair.astype(F32)
-        gskip_ref[:, cols] = colsum(dscan * pair32)
+        by_lane = colsum(dscan * pair32)
         ds16 = dscan.astype(BF)
         parts = []
         for side, h in enumerate((2 * q, 2 * q + 1)):
             decay, srow = mixes[h], step_t[h:h + 1, :]
             mine = jnp.where(left if side == 0 else jnp.logical_not(left), pair32, 0.0).astype(BF)
             dmix = dot_nt(ds16, mine) * decay
+            half = jnp.where(left if side == 0 else jnp.logical_not(left), by_lane, 0.0)
+            dskip = dskip + jnp.where(lane == h, jnp.sum(half, axis=1, keepdims=True), 0.0)
             dinter = dinter + dmix * srow
             wide = dmix * inter
             per_source = colsum(wide)
@@ -412,7 +458,14 @@
             dlog_rows.append(-per_source * srow)
             dlog = dlog + jnp.where(lane == h, jnp.sum(wide * srow, axis=1, keepdims=True), 0.0)
             parts.append(dot_tn((inter * decay * srow).astype(BF), ds16))
-        dact[:, cols] = jnp.where(left, parts[0], parts[1]) + dscan * skip_ref[:, cols]
+        dact[:, cols] = jnp.where(left, parts[0], parts[1]) + dscan * skip_of(q)
+    def spread_dproj(part, cols):
+        return [
+            go(dproj.at[:, cols], dp_in.at[i, :, cols], s_p.at[part, i], r_p.at[part, i], group[i][0])
+            for i in range(2)
+        ]
+
+    dp_got = [spread_dproj(0, pl.ds(0, DI))]
     rest = jnp.zeros((T - HEADS, T), F32)
     dstep = jnp.concatenate(dstep_rows + [rest], axis=0).T
     dlog = dlog + jnp.concatenate(dlog_rows + [rest], axis=0).T
@@ -423,149 +476,90 @@
     ddecay = jnp.dot(upper, dlog, precision=lax.Precision.HIGHEST, preferred_element_type=F32)
     dstep = dstep + ddecay * rate
     draw = dstep * jax.nn.sigmoid(step_in)
-    ghead_ref[0:1, :] = colsum(draw)
-    ghead_ref[1:2, :] = colsum(ddecay * step * rate)
+    gs[5:6, 768:896] = colsum(draw)
+    gs[5:6, 896:1024] = colsum(ddecay * step * rate)
+    gs[5:6, 1024:1152] = dskip
     dproj[:, MAIN:] = draw.astype(BF)
+    W = 256
     for k in range(0, CHAN, W):
         cols = slice(k, k + W)
         v, raw = conv[:, cols], ci[:, cols]
         sig = jax.nn.sigmoid(v)
         dconv = dact[:, cols] * (sig * (1.0 + v * (1.0 - sig)))
-        gcb_ref[:, cols] = colsum(dconv)
-        gtaps_ref[KCONV - 1:KCONV, cols] = colsum(dconv * raw)
+        gs[4:5, cols] = colsum(dconv)
+        gs[KCONV - 1:KCONV, cols] = colsum(dconv * raw)
         dci = dconv * taps_ref[KCONV - 1:KCONV, cols]
         for j in range(1, KCONV):
             here = dconv * within[j]
-            gtaps_ref[KCONV - 1 - j:KCONV - j, cols] = colsum(here * pltpu.roll(raw, j, 0))
+            gs[KCONV - 1 - j:KCONV - j, cols] = colsum(here * pltpu.roll(raw, j, 0))
             dci = dci + pltpu.roll(here * taps_ref[KCONV - 1 - j:KCONV - j, cols], T - j, 0)
         dproj[:, DI + k:DI + k + W] = dci.astype(BF)
 
+    dp_got.append(spread_dproj(1, pl.ds(DI, PADC - DI)))
     dn = dot_nt(dproj[:, MAIN:], tail[...])
     for k in range(0, MAIN, 256):
         dn = dn + dot_nt(dproj[:, k:k + 256], wi_ref[:, k:k + 256])
     xr = x * r1
-    gpg_ref[...] = colsum(dn * xr)
+    gs[5:6, 0:D] = colsum(dn * xr)
     u = dn * pg_ref[...]
     dx = r1 * (u - xr * jnp.mean(u * xr, axis=1, keepdims=True)) + dy
     gx_ref[...] = dx.astype(BF)
 
-    def put(shard, chunk, first, value):
+    small_copy = go(gs, srecv.at[0], s_s.at[0], r_s.at[0], core)
+    forwarded = []
+    for part, cols in enumerate((pl.ds(0, DI), pl.ds(DI, PADC - DI))):
+        dp_got[part][1].wait_recv()
+        forwarded.append(go(
+            dp_in.at[1, :, cols], dp_in.at[2, :, cols], s_p.at[part, 2], r_p.at[part, 2], core
+        ))
+        dp_got[part][0].wait_recv()
+    for copy in n_got + d_got + n2_got:
+        copy.wait_recv()
+    n_all = [nt[me]] + [n_in[i] for i in range(3)]
+    n2_all = [n2t[me]] + [n2_in[i] for i in range(3)]
+    d_all = [d_own] + [d_in.at[i] for i in range(3)]
+    dp_all = [dproj] + [dp_in.at[i] for i in range(3)]
+
+    def put(chunk, first, value):
         wide = value.shape[1]
-        g_ref[shard, :, chunk, :, first:first + wide] = value.astype(BF).reshape(PIECES, PR, wide)
-
-    for s in range(4):
-        left_rows = nt[192 * s:192 * s + 192, :]
-        for k in range(5):
-            put(s, k, 0, dot(left_rows, dproj[:, CW * k:CW * k + CW]))
-        put(s, 5, 0, dot(left_rows, dproj[:, 5 * CW:]))
-        rows_a = n2t[384 * s:384 * s + 192, :]
-        rows_b = n2t[384 * s + 192:384 * s + 384, :]
-        put(s, 5, 256, dot(rows_a, d16[:, :384]))
-        put(s, 6, 0, dot(rows_a, d16[:, 384:]))
-        put(s, 6, 384, dot(rows_b, d16[:, :256]))
-        put(s, 7, 0, dot(rows_b, d16[:, 256:]))
-        put(s, 7, 512, jnp.zeros((192, 128), F32))
-
-
-def layer(tokens, cotangent, lens, w_in, w_out, taps, cb, head, skip, pg, gg):
-    vmem = pl.BlockSpec(memory_space=pltpu.VMEM)
-    shape = jax.ShapeDtypeStruct
-    return pl.pallas_call(
-        layer_kernel,
-        out_shape=(
-            shape((T, D), BF), shape((T, D), BF), shape((4, PIECES, CH, PR, CW), BF),
-            shape((KCONV, CHAN), F32), shape((1, CHAN), F32), shape((2, 128), F32),
-            shape((1, DI), F32), shape((1, D), F32), shape((1, DI), F32),
-        ),
-        in_specs=[vmem, vmem, pl.BlockSpec(memory_space=pltpu.SMEM)] + [vmem] * 8,
-        out_specs=[vmem] * 9,
-        scratch_shapes=[
-            pltpu.VMEM((T, DI), F32), pltpu.VMEM((T, CHAN), F32), pltpu.VMEM((T, CHAN), F32),
-            pltpu.VMEM((T, CHAN), BF), pltpu.VMEM((T, DI), F32), pltpu.VMEM((HEADS, T, T), F32),
-            pltpu.VMEM((T, PADC), BF), pltpu.VMEM((D, 128), BF), pltpu.VMEM((D, T), BF),
-            pltpu.VMEM((DI, T), BF), pltpu.VMEM((T, DI), F32), pltpu.VMEM((T, D), BF),
-            pltpu.VMEM((T, DI), F32), pltpu.VMEM((T, CHAN), F32),
-        ],
-        compiler_params=pltpu.CompilerParams(vmem_limit_bytes=VMEM_BYTES),
-        name="layer",
-    )(tokens, cotangent, lens, w_in, w_out, taps, cb, head, skip, pg, gg)
-
-
-def reduce_kernel(
-    g, sm, red, sm_out, own, rc, r1, r2, rz, sbuf, srecv,
-    loc, s_c, r_c, s_1, r_1, s_2, r_2, s_z, r_z, s_g, r_g, s_x, r_x, s_s, r_s,
-):
-    z, x, y, c = place()
-    core, other_y, other_x = target(z, x, y, 1 - c), target(z, x, 1 - y, c), target(z, 1 - x, y, c)
-    others = [lax.rem(z + d, 4) for d in (1, 2, 3)]
-    over_z = [target(o, x, y, c) for o in others]
-    greet([core, other_y, other_x] + over_z)
-    started = []
-
-    def go(*args):
-        copy = send(*args)
-        started.append(copy)
-        return copy
-
-    mine, away = pl.ds(4 * x, 4), pl.ds(4 * (1 - x), 4)
-    first = []
-    small_copy = go(sm, srecv.at[0], s_s.at[0], r_s.at[0], core)
-    for p in range(PIECES):
-        first.append([
-            go(g.at[2 * i + 1 - c, p], rc.at[i, p], s_c.at[p, i], r_c.at[p, i], core) for i in range(2)
-        ])
-    keep = [
-        [pltpu.make_async_copy(g.at[2 * i + c, p], own.at[i, p], loc.at[p, i]) for i in range(2)]
-        for p in range(PIECES)
-    ]
-    for pair in keep:
-        for copy in pair:
-            copy.start()
-
-    def add(dst, src, chunks):
-        def step(i, carry):
-            a, b = dst.at[i], src.at[i]
-            a[...] = (a[...].astype(F32) + b[...].astype(F32)).astype(BF)
-            return carry
-
-        lax.fori_loop(0, chunks, step, 0)
-
-    second = []
-    for p in range(PIECES):
-        for i in range(2):
-            keep[p][i].wait()
-            first[p][i].wait_recv()
-            add(own.at[i, p], rc.at[i, p], CH)
-        if p % 2 == 0:
-            second.append([go(own.at[1 - y, p], r1.at[p], s_1.at[p, 0], r_1.at[p, 0], other_y)])
-        else:
-            second.append([
-                go(own.at[i, p, away], r1.at[p, pl.ds(4 * i, 4)], s_1.at[p, i], r_1.at[p, i], other_x)
-                for i in range(2)
-            ])
+        own[:, chunk, :, first:first + wide] = value.astype(BF).reshape(PIECES, PR, wide)
+
+    def total(lefts, rights, cols):
+        value = dot(lefts[0], rights[0][:, cols])
+        for a, b in zip(lefts[1:], rights[1:]):
+            value = value + dot(a, b[:, cols])
+        return value
+
+    rows_a, rows_b = [v[:192] for v in n2_all], [v[192:] for v in n2_all]
+    put(5, 256, total(rows_a, d_all, slice(0, 384)))
+    put(6, 0, total(rows_a, d_all, slice(384, 768)))
+    put(6, 384, total(rows_b, d_all, slice(0, 256)))
+    put(7, 0, total(rows_b, d_all, slice(256, 768)))
+    put(7, 512, jnp.zeros((192, 128), F32))
     small_copy.wait_recv()
-    sbuf[0] = sm[...] + srecv[0]
+    sbuf[0] = gs[...] + srecv[0]
     small_copy = go(sbuf.at[0], srecv.at[1], s_s.at[1], r_s.at[1], other_y)
-    third = []
-    for p in range(PIECES):
-        for copy in second[p]:
-            copy.wait_recv()
-        if p % 2 == 0:
-            add(own.at[y, p], r1.at[p], CH)
-            third.append(go(own.at[y, p, away], r2.at[p], s_2.at[p], r_2.at[p], other_x))
-        else:
-            for i in range(2):
-                add(own.at[i, p, mine], r1.at[p, pl.ds(4 * i, 4)], 4)
-            third.append(go(own.at[1 - y, p, mine], r2.at[p], s_2.at[p], r_2.at[p], other_y))
+    forwarded[0].wait_recv()
+    for k in range(2):
+        put(k, 0, total(n_all, dp_all, slice(CW * k, CW * k + CW)))
+    forwarded[1].wait_recv()
+    for k in range(2, 5):
+        put(k, 0, total(n_all, dp_all, slice(CW * k, CW * k + CW)))
+    put(5, 0, total(n_all, dp_all, slice(5 * CW, PADC)))
+
+    mine, away = pl.ds(4 * x_at, 4), pl.ds(4 * (1 - x_at), 4)
+    halves = [go(own.at[p, away], half_in.at[p], s_h.at[p], r_h.at[p], other_x) for p in range(PIECES)]
     small_copy.wait_recv()
     sbuf[1] = sbuf[0] + srecv[1]
     small_copy = go(sbuf.at[1], srecv.at[2], s_s.at[2], r_s.at[2], other_x)
     spread = []
     for p in range(PIECES):
-        third[p].wait_recv()
-        add(own.at[y, p, mine], r2.at[p], 4)
+        halves[p].wait_recv()
+        for i in range(4):
+            at = own.at[p, 4 * x_at + i]
+            at[...] = (at[...].astype(F32) + half_in[p, i].astype(F32)).astype(BF)
         spread.append([
-            go(own.at[y, p, 4 * x + others[d]], rz.at[p, d], s_z.at[p, d], r_z.at[p, d], over_z[d])
+            go(own.at[p, 4 * x_at + others[d]], rz.at[p, d], s_z.at[p, d], r_z.at[p, d], over_z[d])
             for d in range(3)
         ])
     small_copy.wait_recv()
@@ -575,11 +569,11 @@
     for p in range(PIECES):
         for copy in spread[p]:
             copy.wait_recv()
-        total = own[y, p, 4 * x + z].astype(F32)
+        value = own[p, 4 * x_at + z].astype(F32)
         for d in range(3):
-            total = total + rz[p, d].astype(F32)
-        at = red.at[p, 4 * x + z]
-        at[...] = total.astype(BF)
+            value = value + rz[p, d].astype(F32)
+        at = red.at[p, 4 * x_at + z]
+        at[...] = value.astype(BF)
         back.append([go(at, at, s_g.at[p, d], r_g.at[p, d], over_z[d]) for d in range(3)])
     last = []
     for p in range(PIECES):
@@ -590,55 +584,62 @@
     for copy in small:
         copy.wait_recv()
     pieces = [sbuf[2], srecv[3], srecv[4], srecv[5]]
-    here = jnp.zeros(here_shape, F32)
+    value = jnp.zeros(gs.shape, F32)
     for zi in range(4):
         back_by = lax.rem(z - zi + 4, 4)
         pick = pieces[0]
         for d in (1, 2, 3):
             pick = jnp.where(back_by == d, pieces[d], pick)
-        here = here + pick
-    mine_rows = jnp.where(y == 0, jnp.where(c == 0, here[0], here[1]), jnp.where(c == 0, here[2], here[3]))
-    sm_out[...] = mine_rows
+        value = value + pick
+    sm_out[...] = value
     for copy in last:
         copy.wait_recv()
     for copy in started:
         copy.wait_send()
 
 
-here_shape = (4, SROWS, 128)
-
-
-def reduce_grads(g, small):
+def layer(tokens, cotangent, lens, w_in, w_out, params):
+    vmem = pl.BlockSpec(memory_space=pltpu.VMEM)
+    shape = jax.ShapeDtypeStruct
     dma = pltpu.SemaphoreType.DMA
-    vmem = pl.BlockSpec(memory_space=pltpu.VMEM)
     return pl.pallas_call(
-        reduce_kernel,
+        layer_kernel,
         out_shape=(
-            jax.ShapeDtypeStruct((PIECES, CH, PR, CW), BF),
-            jax.ShapeDtypeStruct((SROWS, 128), F32),
+            shape((T, D), BF), shape((T, D), BF), shape((PIECES, CH, PR, CW), BF), shape((8, CHAN), F32),
         ),
-        in_specs=[pl.BlockSpec(memory_space=pl.ANY), vmem],
-        out_specs=[vmem, vmem],
+        in_specs=[vmem, vmem, pl.BlockSpec(memory_space=pltpu.SMEM)] + [vmem] * 3,
+        out_specs=[vmem] * 4,
         scratch_shapes=[
-            pltpu.VMEM((2, PIECES, CH, PR, CW), BF), pltpu.VMEM((2, PIECES, CH, PR, CW), BF),
+            pltpu.VMEM((T, DI), F32), pltpu.VMEM((T, CHAN), F32), pltpu.VMEM((T, CHAN), F32),
+            pltpu.VMEM((T, CHAN), BF), pltpu.VMEM((T, DI), F32), pltpu.VMEM((HEADS, T, T), F32),
+            pltpu.VMEM((T, PADC), BF), pltpu.VMEM((D, 128), BF), pltpu.VMEM((4, 192, T), BF),
+            pltpu.VMEM((4, 384, T), BF), pltpu.VMEM((T, DI), F32), pltpu.VMEM((T, D), BF),
+            pltpu.VMEM((T, DI), F32), pltpu.VMEM((T, CHAN), F32),
+            pltpu.VMEM((4, 384, D), BF), pltpu.VMEM((T, D), BF), pltpu.VMEM((3, T, D), BF),
+            pltpu.VMEM((3, 192, T), BF), pltpu.VMEM((3, 384, T), BF), pltpu.VMEM((3, T, PADC), BF),
             pltpu.VMEM((PIECES, CH, PR, CW), BF), pltpu.VMEM((PIECES, 4, PR, CW), BF),
-            pltpu.VMEM((PIECES, 3, PR, CW), BF),
-            pltpu.VMEM((3, 4, SROWS, 128), F32), pltpu.VMEM((6, 4, SROWS, 128), F32),
-            dma((PIECES, 2)), dma((PIECES, 2)), dma((PIECES, 2)), dma((PIECES, 2)), dma((PIECES, 2)),
-            dma((PIECES,)), dma((PIECES,)), dma((PIECES, 3)), dma((PIECES, 3)), dma((PIECES, 3)),
-            dma((PIECES, 3)), dma((PIECES,)), dma((PIECES,)), dma((6,)), dma((6,)),
+            pltpu.VMEM((PIECES, 3, PR, CW), BF), pltpu.VMEM((8, CHAN), F32),
+            pltpu.VMEM((3, 8, CHAN), F32), pltpu.VMEM((6, 8, CHAN), F32),
+            dma((5,)), dma((5,)), dma((3,)), dma((3,)), dma((3,)), dma((3,)), dma((3,)), dma((3,)),
+            dma((2, 3)), dma((2, 3)), dma((PIECES,)), dma((PIECES,)), dma((PIECES, 3)), dma((PIECES, 3)),
+            dma((PIECES, 3)), dma((PIECES, 3)), dma((PIECES,)), dma((PIECES,)), dma((6,)), dma((6,)),
         ],
         compiler_params=pltpu.CompilerParams(
             collective_id=1, has_side_effects=True, vmem_limit_bytes=VMEM_BYTES
         ),
-        name="reduce_grads",
-    )(g, small)
+        name="layer",
+    )(tokens, cotangent, lens, w_in, w_out, params)
 
 
 def adamw_kernel(red, wi, mi, vi, wo, mo, vo, nwi, nmi, nvi, nwo, nmo, nvo):
     def update(cols, grad, refs, rate, part=None):
         at = (slice(None), cols) if part is None else (part, slice(None), cols)
-        new = adamw(refs[0][at], grad.astype(F32), refs[1][at], refs[2][at], rate, 0.1)
+        gradient, master = grad.astype(F32), refs[0][at].astype(F32)
+        first = beta_one * refs[1][at] + (1.0 - beta_one) * gradient
+        second = beta_two * refs[2][at] + (1.0 - beta_two) * gradient * gradient
+        root = jnp.sqrt(second * (1.0 / (1.0 - beta_two**STEP))) + adam_eps
+        scale = rate / (1.0 - beta_one**STEP)
+        new = (master * (1.0 - rate * 0.1) - scale * first / root, first, second)
         for ref, value in zip(refs[3:], new):
             ref[at] = value
 
@@ -676,28 +677,24 @@
 ):
     share = w_small.shape[0]
     small = jnp.pad(w_small, (0, 32 * 128 - share)).reshape(32, 128)
-    full_in, full_out, full_small = gather_weights(w_in, w_out, small)
+    full_in, full_small = gather_weights(w_in, small)
     packed = full_small.reshape(4, 32 * 128)[:, :share].reshape(4 * share).astype(F32)
     start = (KCONV + 1) * CHAN
-    taps = packed[: KCONV * CHAN].reshape(KCONV, CHAN)
-    cb = packed[KCONV * CHAN : start].reshape(1, CHAN)
-    head = jnp.pad(packed[start : start + 2 * HEADS].reshape(2, HEADS), ((0, 0), (0, 128 - HEADS)))
-    skip = jnp.repeat(packed[start + 2 * HEADS : start + 3 * HEADS], HEAD).reshape(1, DI)
     gains = start + 3 * HEADS
-    pg = packed[gains : gains + D].reshape(1, D)
-    gg = packed[gains + D :].reshape(1, DI)
-    out, gx, g, gtaps, gcb, ghead, gskip, gpg, ggg = layer(
-        tokens, cotangent, seq_lengths, full_in.reshape(D, CIN), full_out.reshape(DI, D),
-        taps, cb, head, skip, pg, gg,
+    heads = jnp.pad(packed[start:gains].reshape(3, HEADS), ((0, 0), (0, 128 - HEADS)))
+    params = jnp.concatenate([
+        packed[:start], packed[gains : gains + D], heads.reshape(-1), jnp.zeros(CHAN - D - 384, F32),
+        packed[gains + D :], jnp.zeros(2 * CHAN - DI, F32),
+    ]).reshape(8, CHAN)
+    out, gx, red, sums = layer(
+        tokens, cotangent, seq_lengths, full_in.reshape(D, CIN), w_out, params
     )
     flat = jnp.concatenate([
-        gtaps.reshape(-1), gcb.reshape(-1), ghead[:, :HEADS].reshape(-1),
-        gskip.reshape(HEADS, HEAD).sum(axis=1), gpg.reshape(-1), ggg.reshape(-1),
+        sums[:5].reshape(-1), sums[5, D : D + HEADS], sums[5, D + 128 : D + 128 + HEADS],
+        sums[5, D + 256 : D + 256 + HEADS], sums[5, :D], sums[6, :DI],
     ])
-    flat = jnp.pad(flat.reshape(4, share), ((0, 0), (0, SROWS * 128 - share))).reshape(4, SROWS, 128)
-    red, small_sum = reduce_grads(g, flat)
+    share_small = lax.dynamic_slice_in_dim(flat, lax.axis_index("shard") * share, share)
     new = adamw_all(red, w_in, m_in, v_in, w_out, m_out, v_out)
-    share_small = small_sum.reshape(-1)[:share]
     new_small = adamw(w_small, share_small, m_small, v_small, 0.3, 0.0)
     return (out, gx, *new, *new_small)
 

time: 208 us -> 190 us (0.913)
  Pallas kernels: 193 us -> 178 us
  other arithmetic: 4.3 us -> 0.72 us
    pallas_call x1, Pallas kernels: 16.3 us -> 120 us  [layer(): pl.pallas_call(layer_kernel, out_shape=(shape((T, D), BF), shape((T, D),...]
    pallas_call x1 -> x0, Pallas kernels: 101 us -> none  [reduce_grads(): pl.pallas_call(reduce_kernel, out_shape=(jax.ShapeDtypeStruct((PIECES, CH...]
    pallas_call x1, Pallas kernels: 62.8 us -> 44.9 us  [gather_weights(): pl.pallas_call(gather_kernel, out_shape=(jax.ShapeDtypeStruct((4, 192, CI...]
    pallas_call x4 -> x0, other arithmetic: 2.84 us -> none  [layer(): pl.pallas_call(layer_kernel, out_shape=(shape((T, D), BF), shape((T, D),...]
    reshape x9 -> x3, local copies, waits for them, and re-layouts: 4.11 us -> 1.55 us  [the longest x1 0.83 us: on_device_fast(): sums[:5].reshape(-1)]
where the time goes in v2:
time: 190 us; the launch traced here: 187 us
  Pallas kernels  178 us (94%)
  local copies, waits for them, and re-layouts  7.61 us (4%)
    pallas_call x1, Pallas kernels, layer(): pl.pallas_call(layer_kernel, out_shape=(shape((T, D), BF), shape((T, D),...  120 us
    pallas_call x1, Pallas kernels, gather_weights(): pl.pallas_call(gather_kernel, out_shape=(jax.ShapeDtypeStruct((4, 192, CI...  44.9 us
    pallas_call x1, Pallas kernels, adamw_all(): pl.pallas_call(adamw_kernel, grid=(192 // rows,), out_shape=[jax.ShapeDty...  13.4 us

profile of v2, /device:TPU:0, one launch (start us, length us, event | category | flops | bytes accessed | tf_op | source)
XLA Modules:
  0.0 187.3 jit_solution(15448395538111431525)
XLA Ops:
  0.6 1.3 pad_bitcast_fusion.sm
  1.9 44.9 %gather_weights.1 = (bf16[4,192,3352]{2,1,0:T(8,128)(2,1)}, bf16[4,32,128]{2,1,0:T(8,128)(2,1)}) custom-call(bf16[192,3352]{1,0:T(8,128)(2,1)} %wi.3, bf16[32,128]{1,0:T(8,128)(2,1)} %pad_bitcast_fusion.sm), custom_call_target="tpu_custom_call" | custom-call | tf_op jit(solution)/shard_map/gather_weights/pallas_call | solution.py:264
  46.8 0.8 copy.25
  47.6 0.1 reshape.77
  47.7 0.1 slice_dynamic-update-slice_fusion.2
  47.8 0.1 reshape.67
  47.9 0.1 slice_dynamic-update-slice_fusion.1
  48.0 0.6 reshape.69.par_ref
  48.6 0.0 copy-start.2
  48.6 120.0 %layer.1 = (bf16[128,768]{1,0:T(8,128)(2,1)}, bf16[128,768]{1,0:T(8,128)(2,1)}, bf16[4,8,48,640]{3,2,1,0:T(8,128)(2,1)}, f32[8,1792]{1,0:T(8,128)}) custom-call(bf16[128,768]{1,0:T(8,128)(2,1)} %x_ref.1, bf16[128,768]{1,0:T(8,128)(2,1)} %ct_ref.1, s32[1,4]{1,0:T(1,128)} %len_ref.1, bf16[768,3352]{1,0:T(8,128)(2,1)} %bitcast.22, bf16[384,768]{1,0:T(8,128)(2,1)} %wo_own.1, ...), custom_call_target="tpu_custom_call" | custom-call | tf_op jit(solution)/shard_map/layer/pallas_call | solution.py:605
  168.6 0.7 slice_bitcast_fusion
  169.3 0.8 slice_reduce_fusion.1
  170.0 0.8 slice_reduce_fusion
  170.9 0.8 reshape.76
  171.7 0.1 concatenate.7
  171.8 0.0 copy-done.2
  171.8 0.0 copy-done.3
  171.8 0.0 copy-done.4
  171.8 0.7 convert_subtract_fusion
  172.5 13.4 %adamw.1 = (f32[192,3352]{1,0:T(8,128)}, f32[192,3352]{1,0:T(8,128)}, f32[192,3352]{1,0:T(8,128)}, f32[2,192,768]{2,1,0:T(8,128)}, f32[2,192,768]{2,1,0:T(8,128)}, /*index=5*/f32[2,192,768]{2,1,0:T(8,128)}) custom-call(bf16[4,8,48,640]{3,2,1,0:T(8,128)(2,1)} %get-tuple-element.27.red, bf16[192,3352]{1,0:T(8,128)(2,1)} %wi.3, f32[192,3352]{1,0:T(8,128)} %mi.1, ...), custom_call_target="tpu_custom_call" | custom-call | tf_op jit(solution)/shard_map/adamw/pallas_call | solution.py:662
  185.9 0.0 copy-done.1
  185.9 0.7 copy.34
  186.6 0.0 copy-done
  186.6 0.7 copy.35
  (11 shorter events, 0.0 us)
Async XLA Ops:
  48.6 123.2 %copy-start.2 = (bf16[2834]{0:T(1024)(128)(2,1)S(1)}, bf16[2834]{0:T(1024)(128)(2,1)}, u32[]{:S(2)}) copy-start(bf16[2834]{0:T(1024)(128)(2,1)} %param.17) | copy-start | bytes 17008
  48.6 123.2 %copy-start.3 = (f32[2834]{0:T(1024)S(1)}, f32[2834]{0:T(1024)}, u32[]{:S(2)}) copy-start(f32[2834]{0:T(1024)} %param.22) | copy-start | bytes 34012
  48.6 123.2 %copy-start.4 = (f32[2834]{0:T(1024)S(1)}, f32[2834]{0:T(1024)}, u32[]{:S(2)}) copy-start(f32[2834]{0:T(1024)} %param.23) | copy-start | bytes 34012
  172.5 13.4 %copy-start.1 = (bf16[128,768]{1,0:T(8,128)(2,1)S(1)}, bf16[128,768]{1,0:T(8,128)(2,1)}, u32[]{:S(2)}) copy-start(bf16[128,768]{1,0:T(8,128)(2,1)} %get-tuple-element.52) | copy-start | bytes 589828
  172.5 14.1 %copy-start = (bf16[128,768]{1,0:T(8,128)(2,1)S(1)}, bf16[128,768]{1,0:T(8,128)(2,1)}, u32[]{:S(2)}) copy-start(bf16[128,768]{1,0:T(8,128)(2,1)} %get-tuple-element.53) | copy-start | bytes 589828

commit v3 on v2

--- a/solution.py
+++ b/solution.py
@@ -190,7 +190,8 @@
 CW = 640
 SROWS = 24
 MESH = pl.DeviceIdType.MESH
-VMEM_BYTES = 58 * 1024 * 1024
+VMEM_BYTES = 24 * 1024 * 1024
+LAYER_BYTES = 40 * 1024 * 1024
 BF = jnp.bfloat16
 F32 = jnp.float32
 
@@ -220,43 +221,46 @@
     return copy
 
 
-def gather_kernel(wi, sm, fi, fs, loc, s_own, r_own, s_y, r_y, s_x, r_x, s_fy, r_fy, s_fx, r_fx):
+def gather_kernel(wi, sm, fi, fs, loc, s_own, r_own, s_y, r_y, s_x, r_x, s_sm, r_sm):
     z, x, y, c = place()
-    core, other_y, other_x = target(z, x, y, 1 - c), target(z, x, 1 - y, c), target(z, 1 - x, y, c)
-    greet((core, other_y, other_x))
-    me, far = 2 * y + c, 2 * (1 - y) + c
-    over_y = [send(sm, fs.at[me], s_y.at[3], r_y.at[3], other_y)]
-    own = [send(sm, fs.at[me], s_own.at[1], r_own.at[1], core)]
-    for u in range(3):
-        here = pl.ds(pl.multiple_of(x * 96 + 32 * u, 16), 32)
-        over_y.append(send(wi.at[here], fi.at[me, here], s_y.at[u], r_y.at[u], other_y))
-    own.append(send(wi, fi.at[me], s_own.at[0], r_own.at[0], core))
+    core, other_y = target(z, x, y, 1 - c), target(z, x, 1 - y, c)
+    diag, other_x = target(z, x, 1 - y, 1 - c), target(z, 1 - x, y, c)
+    greet((core, other_y, diag, other_x))
+    me = 2 * y + c
+    far = (2 * (1 - y) + c, 2 * (1 - y) + 1 - c)
+    small = [
+        send(sm, fs.at[me], s_sm.at[i], r_sm.at[i], peer) for i, peer in enumerate((core, other_y, diag))
+    ]
+    over_y = []
+    for u in range(GATHER):
+        here = pl.ds(pl.multiple_of(x * 96 + 96 // GATHER * u, 16), 96 // GATHER)
+        over_y.append([
+            send(wi.at[here], fi.at[me, here], s_y.at[u, i], r_y.at[u, i], peer)
+            for i, peer in enumerate((other_y, diag))
+        ])
+    own = send(wi, fi.at[me], s_own.at[0], r_own.at[0], core)
     keep = [
         pltpu.make_async_copy(src, full.at[me], loc.at[i])
         for i, (src, full) in enumerate(((wi, fi), (sm, fs)))
     ]
     for copy in keep:
         copy.start()
-    over_x, on_y, on_x = [], [], []
-    over_y[0].wait_recv()
-    on_y.append(send(fs.at[far], fs.at[far], s_fy.at[3], r_fy.at[3], core))
-    for u in range(3):
-        here = pl.ds(pl.multiple_of(x * 96 + 32 * u, 16), 32)
-        over_y[u + 1].wait_recv()
-        part = fi.at[far, here]
-        over_x.append(send(part, part, s_x.at[u], r_x.at[u], other_x))
-        on_y.append(send(part, part, s_fy.at[u], r_fy.at[u], core))
-    for u in range(3):
-        there = pl.ds(pl.multiple_of((1 - x) * 96 + 32 * u, 16), 32)
-        over_x[u].wait_recv()
-        part = fi.at[far, there]
-        on_x.append(send(part, part, s_fx.at[u], r_fx.at[u], core))
+    over_x = []
+    for u in range(GATHER):
+        here = pl.ds(pl.multiple_of(x * 96 + 96 // GATHER * u, 16), 96 // GATHER)
+        for i in range(2):
+            over_y[u][i].wait_recv()
+            part = fi.at[far[i], here]
+            over_x.append(send(part, part, s_x.at[u, i], r_x.at[u, i], other_x))
     for copy in keep:
         copy.wait()
-    for copy in own + on_y + on_x:
+    for copy in small + [own] + over_x:
         copy.wait_recv()
-    for copy in over_y + own + over_x + on_y + on_x:
+    for copy in small + [own] + over_x + [copy for pair in over_y for copy in pair]:
         copy.wait_send()
+
+
+GATHER = 3
 
 
 def gather_weights(w_in, small):
@@ -269,8 +273,8 @@
         ),
         in_specs=[pl.BlockSpec(memory_space=pl.ANY)] * 2,
         out_specs=[pl.BlockSpec(memory_space=pl.ANY)] * 2,
-        scratch_shapes=[dma((2,)), dma((2,)), dma((2,)), dma((4,)), dma((4,)), dma((3,)), dma((3,)),
-                        dma((4,)), dma((4,)), dma((3,)), dma((3,))],
+        scratch_shapes=[dma((2,)), dma((1,)), dma((1,)), dma((GATHER, 2)), dma((GATHER, 2)),
+                        dma((GATHER, 2)), dma((GATHER, 2)), dma((3,)), dma((3,))],
         compiler_params=pltpu.CompilerParams(collective_id=0, has_side_effects=True),
         name="gather_weights",
     )(w_in, small)
@@ -295,9 +299,9 @@
 def layer_kernel(
     x_ref, ct_ref, len_ref, wi_ref, wo_own, par_ref,
     out_ref, gx_ref, red, sm_out,
-    gate, ci, conv, inner, scan, mixes, dproj, tail, nt, n2t, gated, n16, dn2_keep, dact,
-    wo_full, d_own, d_in, n_in, n2_in, dp_in, own, half_in, rz, gs, sbuf, srecv,
-    s_w, r_w, s_d, r_d, s_n, r_n, s_2, r_2, s_p, r_p, s_h, r_h, s_z, r_z, s_g, r_g, s_x, r_x, s_s, r_s,
+    gate, ci, conv, inner, scan, mixes, dproj, tail, nt, n2t, gated, n16, dact,
+    dn2_all, dn2_out, out_part, out_in, d_own, d_in, n_in, n2_in, dp_in, own, half_in, rz, gs, sbuf, srecv,
+    s_o, r_o, s_w, r_w, s_d, r_d, s_n, r_n, s_2, r_2, s_p, r_p, s_h, r_h, s_z, r_z, s_g, r_g, s_x, r_x, s_s, r_s,
 ):
     z, x_at, y, c = place()
     core, other_y = target(z, x_at, y, 1 - c), target(z, x_at, 1 - y, c)
@@ -314,11 +318,6 @@
 
     me, far = 2 * y + c, 2 * (1 - y) + c
     group = [(core, 2 * y + 1 - c), (other_y, far), (diag, 2 * (1 - y) + 1 - c)]
-    here = pl.ds(pl.multiple_of(x_at * 192, 16), 192)
-    there = pl.ds(pl.multiple_of((1 - x_at) * 192, 16), 192)
-    w_over_y = go(wo_own.at[here], wo_full.at[me, here], s_w.at[0], r_w.at[0], other_y)
-    w_own = go(wo_own, wo_full.at[me], s_w.at[1], r_w.at[1], core)
-    wo_full[me] = wo_own[...]
     taps_ref, cb_ref = par_ref.at[0:4], par_ref.at[4:5]
     pg_ref, gg_ref = par_ref.at[5:6, 0:D], par_ref.at[6:7, 0:DI]
     step_bias, decay_log, skips = (par_ref[5:6, 768 + 128 * i:896 + 128 * i] for i in range(3))
@@ -352,8 +351,10 @@
     d_own[...] = d16
     d_got, n_got, n2_got = [], [], []
     for i, (peer, shard) in enumerate(group):
+        d_got.append(go(d_own, d_in.at[i], s_d.at[i], r_d.at[i], peer))
+    for i, (peer, shard) in enumerate(group):
         n_got.append(go(nt.at[shard], n_in.at[i], s_n.at[i], r_n.at[i], peer))
-        d_got.append(go(d_own, d_in.at[i], s_d.at[i], r_d.at[i], peer))
+    dn2_all[me] = dot_nt(d16, wo_own[...]).astype(BF)
     tail[...] = jnp.zeros(tail.shape, BF)
     tail[:, :HEADS] = wi_ref[:, MAIN:]
     n = n16[...]
@@ -370,10 +371,11 @@
             total = total + taps_ref[KCONV - 1 - j:KCONV - j, cols] * pltpu.roll(v, j, 0) * within[j]
         conv[:, cols] = total
         inner[:, cols] = (total * jax.nn.sigmoid(total)).astype(BF)
-    w_over_y.wait_recv()
-    part = wo_full.at[far, here]
-    w_over_x = go(part, part, s_w.at[2], r_w.at[2], other_x)
-    w_fwd = go(part, part, s_w.at[3], r_w.at[3], core)
+    dn2_got = []
+    for i, (peer, shard) in enumerate(group):
+        d_got[i].wait_recv()
+        dn2_out[i] = dot_nt(d_in[i], wo_own[...]).astype(BF)
+        dn2_got.append(go(dn2_out.at[i], dn2_all.at[me], s_w.at[i], r_w.at[i], peer))
     step = jnp.maximum(step_in, 0.0) + jnp.log1p(jnp.exp(-jnp.abs(step_in)))
     rate = -jnp.exp(decay_log)
     tri = (row >= lane).astype(F32)
@@ -404,29 +406,22 @@
         gsq = gsq + jnp.sum(value * value, axis=1, keepdims=True)
     r2 = lax.rsqrt(gsq * (1.0 / DI) + epsilon)
 
-    w_over_x.wait_recv()
-    part = wo_full.at[far, there]
-    w_last = go(part, part, s_w.at[4], r_w.at[4], core)
-    for copy in (w_own, w_fwd, w_last):
+    for k in range(0, DI, 128):
+        n2t[k // 384, k % 384:k % 384 + 128, :] = (
+            gated[:, k:k + 128] * r2 * gg_ref[:, k:k + 128]
+        ).T.astype(BF)
+    for i, (peer, shard) in enumerate(group):
+        n2_got.append(go(n2t.at[shard], n2_in.at[i], s_2.at[i], r_2.at[i], peer))
+    for copy in dn2_got:
         copy.wait_recv()
-    out = x
     mean_ug = jnp.zeros((T, 1), F32)
     W = 128
     for k in range(0, DI, W):
         cols = slice(k, k + W)
         g = gated[:, cols]
-        two = g * r2 * gg_ref[:, cols]
-        two16 = two.astype(BF)
-        w_part = wo_full[k // 384, k % 384:k % 384 + W, :]
-        n2t[k // 384, k % 384:k % 384 + W, :] = two.T.astype(BF)
-        out = out + dot(two16, w_part)
-        dn2 = dot_nt(d16, w_part)
+        dn2 = dn2_all[k // 384, :, k % 384:k % 384 + W].astype(F32)
         gs[6:7, cols] = colsum(dn2 * (g * r2))
         mean_ug = mean_ug + jnp.sum(dn2 * gg_ref[:, cols] * g, axis=1, keepdims=True)
-        dn2_keep[:, cols] = dn2
-    out_ref[...] = out.astype(BF)
-    for i, (peer, shard) in enumerate(group):
-        n2_got.append(go(n2t.at[shard], n2_in.at[i], s_2.at[i], r_2.at[i], peer))
     back = mean_ug * (1.0 / DI) * r2 * r2
 
     dinter = jnp.zeros((T, T), F32)
@@ -436,7 +431,7 @@
     for q in range(HEADS // 2):
         cols = slice(128 * q, 128 * q + 128)
         g, value, gt = gate[:, cols], scan[:, cols], gated[:, cols]
-        dgated = r2 * (dn2_keep[:, cols] * gg_ref[:, cols] - gt * back)
+        dgated = r2 * (dn2_all[q // 3, :, 128 * (q % 3):128 * (q % 3) + 128].astype(F32) * gg_ref[:, cols] - gt * back)
         sig = jax.nn.sigmoid(g)
         dscan = dgated * (g * sig)
         dproj[:, cols] = (dgated * value * (sig * (1.0 + g * (1.0 - sig)))).astype(BF)
@@ -466,6 +461,11 @@
         ]
 
     dp_got = [spread_dproj(0, pl.ds(0, DI))]
+    out_got = []
+    for i, (peer, shard) in enumerate(group):
+        n2_got[i].wait_recv()
+        out_part[i] = dot_tn(n2_in[i], wo_own[...]).astype(BF)
+        out_got.append(go(out_part.at[i], out_in.at[i], s_o.at[i], r_o.at[i], peer))
     rest = jnp.zeros((T - HEADS, T), F32)
     dstep = jnp.concatenate(dstep_rows + [rest], axis=0).T
     dlog = dlog + jnp.concatenate(dlog_rows + [rest], axis=0).T
@@ -513,7 +513,7 @@
             dp_in.at[1, :, cols], dp_in.at[2, :, cols], s_p.at[part, 2], r_p.at[part, 2], core
         ))
         dp_got[part][0].wait_recv()
-    for copy in n_got + d_got + n2_got:
+    for copy in n_got:
         copy.wait_recv()
     n_all = [nt[me]] + [n_in[i] for i in range(3)]
     n2_all = [n2t[me]] + [n2_in[i] for i in range(3)]
@@ -592,6 +592,11 @@
             pick = jnp.where(back_by == d, pieces[d], pick)
         value = value + pick
     sm_out[...] = value
+    out = x_ref[...].astype(F32) + dot_tn(n2t[me], wo_own[...])
+    for i in range(3):
+        out_got[i].wait_recv()
+        out = out + out_in[i].astype(F32)
+    out_ref[...] = out.astype(BF)
     for copy in last:
         copy.wait_recv()
     for copy in started:
@@ -614,18 +619,19 @@
             pltpu.VMEM((T, CHAN), BF), pltpu.VMEM((T, DI), F32), pltpu.VMEM((HEADS, T, T), F32),
             pltpu.VMEM((T, PADC), BF), pltpu.VMEM((D, 128), BF), pltpu.VMEM((4, 192, T), BF),
             pltpu.VMEM((4, 384, T), BF), pltpu.VMEM((T, DI), F32), pltpu.VMEM((T, D), BF),
-            pltpu.VMEM((T, DI), F32), pltpu.VMEM((T, CHAN), F32),
-            pltpu.VMEM((4, 384, D), BF), pltpu.VMEM((T, D), BF), pltpu.VMEM((3, T, D), BF),
+            pltpu.VMEM((T, CHAN), F32),
+            pltpu.VMEM((4, T, 384), BF), pltpu.VMEM((3, T, 384), BF), pltpu.VMEM((3, T, D), BF),
+            pltpu.VMEM((3, T, D), BF), pltpu.VMEM((T, D), BF), pltpu.VMEM((3, T, D), BF),
             pltpu.VMEM((3, 192, T), BF), pltpu.VMEM((3, 384, T), BF), pltpu.VMEM((3, T, PADC), BF),
             pltpu.VMEM((PIECES, CH, PR, CW), BF), pltpu.VMEM((PIECES, 4, PR, CW), BF),
             pltpu.VMEM((PIECES, 3, PR, CW), BF), pltpu.VMEM((8, CHAN), F32),
             pltpu.VMEM((3, 8, CHAN), F32), pltpu.VMEM((6, 8, CHAN), F32),
-            dma((5,)), dma((5,)), dma((3,)), dma((3,)), dma((3,)), dma((3,)), dma((3,)), dma((3,)),
+            dma((3,)), dma((3,)), dma((3,)), dma((3,)), dma((3,)), dma((3,)), dma((3,)), dma((3,)), dma((3,)), dma((3,)),
             dma((2, 3)), dma((2, 3)), dma((PIECES,)), dma((PIECES,)), dma((PIECES, 3)), dma((PIECES, 3)),
             dma((PIECES, 3)), dma((PIECES, 3)), dma((PIECES,)), dma((PIECES,)), dma((6,)), dma((6,)),
         ],
         compiler_params=pltpu.CompilerParams(
-            collective_id=1, has_side_effects=True, vmem_limit_bytes=VMEM_BYTES
+            collective_id=1, has_side_effects=True, vmem_limit_bytes=LAYER_BYTES
         ),
         name="layer",
     )(tokens, cotangent, lens, w_in, w_out, params)
@@ -655,7 +661,7 @@
 
 
 def adamw_all(red, w_in, m_in, v_in, w_out, m_out, v_out):
-    rows = 16
+    rows = PR
     halves = [v.reshape(2, 192, D) for v in (w_out, m_out, v_out)]
     spec_in = pl.BlockSpec((rows, CIN), lambda i: (i, 0))
     spec_out = pl.BlockSpec((2, rows, D), lambda i: (0, i, 0))
@@ -663,7 +669,7 @@
         adamw_kernel,
         grid=(192 // rows,),
         out_shape=[jax.ShapeDtypeStruct((192, CIN), F32)] * 3 + [jax.ShapeDtypeStruct((2, 192, D), F32)] * 3,
-        in_specs=[pl.BlockSpec((1, CH, rows, CW), lambda i: (i // 3, 0, i % 3, 0))]
+        in_specs=[pl.BlockSpec((1, CH, rows, CW), lambda i: (i, 0, 0, 0))]
         + [spec_in] * 3 + [spec_out] * 3,
         out_specs=[spec_in] * 3 + [spec_out] * 3,
         compiler_params=pltpu.CompilerParams(vmem_limit_bytes=VMEM_BYTES),

time: 190 us -> 194 us (1.021)
  local copies, waits for them, and re-layouts: 7.61 us -> 17.5 us
  Pallas kernels: 178 us -> 173 us
    unnamed x18 -> x44, local copies, waits for them, and re-layouts: 2.33 us -> 15 us
    pallas_call x1, Pallas kernels: 13.4 us -> 5.12 us  [adamw_all(): pl.pallas_call(adamw_kernel, grid=(192 // rows,), out_shape=[jax.ShapeDty...]
    pallas_call x1, Pallas kernels: 120 us -> 123 us  [layer(): pl.pallas_call(layer_kernel, out_shape=(shape((T, D), BF), shape((T, D),...]
where the time goes in v3:
time: 194 us; the launch traced here: 193 us
  Pallas kernels  173 us (89%)
  local copies, waits for them, and re-layouts  17.5 us (9%)
    pallas_call x1, Pallas kernels, layer(): pl.pallas_call(layer_kernel, out_shape=(shape((T, D), BF), shape((T, D),...  123 us
    pallas_call x1, Pallas kernels, gather_weights(): pl.pallas_call(gather_kernel, out_shape=(jax.ShapeDtypeStruct((4, 192, CI...  44.9 us
    unnamed x44, local copies, waits for them, and re-layouts  15 us
    pallas_call x1, Pallas kernels, adamw_all(): pl.pallas_call(adamw_kernel, grid=(192 // rows,), out_shape=[jax.ShapeDty...  5.12 us

profile of v3, /device:TPU:0, one launch (start us, length us, event | category | flops | bytes accessed | tf_op | source)
XLA Modules:
  0.0 193.2 jit_solution(4107208032288728901)
XLA Ops:
  0.7 1.4 pad_bitcast_fusion.sm
  2.1 44.9 %gather_weights.1 = (bf16[4,192,3352]{2,1,0:T(8,128)(2,1)}, bf16[4,32,128]{2,1,0:T(8,128)(2,1)}) custom-call(bf16[192,3352]{1,0:T(8,128)(2,1)} %wi.3, bf16[32,128]{1,0:T(8,128)(2,1)} %pad_bitcast_fusion.sm), custom_call_target="tpu_custom_call" | custom-call | tf_op jit(solution)/shard_map/gather_weights/pallas_call | solution.py:268
  46.9 0.8 copy.25
  47.7 0.1 reshape.77
  47.8 0.1 slice_dynamic-update-slice_fusion.2
  47.9 0.1 reshape.67
  48.0 0.1 slice_dynamic-update-slice_fusion.1
  48.2 2.5 %copy-done = bf16[4,192,3352]{2,1,0:T(8,128)(2,1)S(1)} copy-done((bf16[4,192,3352]{2,1,0:T(8,128)(2,1)S(1)}, bf16[4,192,3352]{2,1,0:T(8,128)(2,1)}, u32[]{:S(2)}) %copy-start) | copy-done | bytes 5148696
  50.6 0.7 copy-done.16
  51.3 123.4 %layer.1 = (bf16[128,768]{1,0:T(8,128)(2,1)S(1)}, bf16[128,768]{1,0:T(8,128)(2,1)S(1)}, bf16[4,8,48,640]{3,2,1,0:T(8,128)(2,1)S(1)}, f32[8,1792]{1,0:T(8,128)S(1)}) custom-call(bf16[128,768]{1,0:T(8,128)(2,1)S(1)} %copy-done.9, bf16[128,768]{1,0:T(8,128)(2,1)S(1)} %copy-done.10, s32[1,4]{1,0:T(1,128)S(1)} %copy-done.16, bf16[768,3352]{1,0:T(8,128)(2,1)S(1)} %bitcast.22, ...), custom_call_target="tpu_custom_call" | custom-call | tf_op jit(solution)/shard_map/layer/pallas_call | solution.py:610
  174.8 1.3 copy-done.5
  176.0 0.7 copy-done.11
  176.7 0.7 copy-done.13
  177.4 0.6 copy-done.15
  178.0 0.8 reshape.76
  178.8 0.1 concatenate.7
  178.9 1.4 convert_subtract_fusion
  180.4 1.7 copy-done.2
  182.1 1.7 copy-done.3
  183.9 1.5 copy-done.6
  185.4 1.3 copy-done.8
  186.7 5.1 %adamw.1 = (f32[192,3352]{1,0:T(8,128)}, f32[192,3352]{1,0:T(8,128)}, f32[192,3352]{1,0:T(8,128)}, f32[2,192,768]{2,1,0:T(8,128)}, f32[2,192,768]{2,1,0:T(8,128)}, /*index=5*/f32[2,192,768]{2,1,0:T(8,128)}) custom-call(bf16[4,8,48,640]{3,2,1,0:T(8,128)(2,1)S(1)} %copy-done.6, bf16[192,3352]{1,0:T(8,128)(2,1)S(1)} %copy-done.1, f32[192,3352]{1,0:T(8,128)S(1)} %copy-done.2, ...), custom_call_target="tpu_custom_call" | custom-call | tf_op jit(solution)/shard_map/adamw/pallas_call | solution.py:668
  191.8 0.7 copy.34
  192.5 0.7 copy.35
  (37 shorter events, 0.1 us)
Async XLA Ops:
  0.6 47.5 %copy-start.4 = (bf16[384,768]{1,0:T(8,128)(2,1)S(1)}, bf16[384,768]{1,0:T(8,128)(2,1)}, u32[]{:S(2)}) copy-start(bf16[384,768]{1,0:T(8,128)(2,1)} %wo_own.1) | copy-start | bytes 1769476
  0.7 47.5 %copy-start.10 = (bf16[128,768]{1,0:T(8,128)(2,1)S(1)}, bf16[128,768]{1,0:T(8,128)(2,1)}, u32[]{:S(2)}) copy-start(bf16[128,768]{1,0:T(8,128)(2,1)} %ct_ref.1) | copy-start | bytes 589828
  0.7 47.5 %copy-start.9 = (bf16[128,768]{1,0:T(8,128)(2,1)S(1)}, bf16[128,768]{1,0:T(8,128)(2,1)}, u32[]{:S(2)}) copy-start(bf16[128,768]{1,0:T(8,128)(2,1)} %x_ref.1) | copy-start | bytes 589828
  48.1 2.5 %copy-start = (bf16[4,192,3352]{2,1,0:T(8,128)(2,1)S(1)}, bf16[4,192,3352]{2,1,0:T(8,128)(2,1)}, u32[]{:S(2)}) copy-start(bf16[4,192,3352]{2,1,0:T(8,128)(2,1)} %get-tuple-element.23) | copy-start | bytes 15446020
  50.6 0.7 copy-start.16
  51.3 127.6 %copy-start.17 = (bf16[2834]{0:T(1024)(128)(2,1)S(1)}, bf16[2834]{0:T(1024)(128)(2,1)}, u32[]{:S(2)}) copy-start(bf16[2834]{0:T(1024)(128)(2,1)} %param.17) | copy-start | bytes 17008
  51.3 129.1 %copy-start.1 = (bf16[192,3352]{1,0:T(8,128)(2,1)S(1)}, bf16[192,3352]{1,0:T(8,128)(2,1)}, u32[]{:S(2)}) copy-start(bf16[192,3352]{1,0:T(8,128)(2,1)} %wi.3) | copy-start | bytes 3861508
  51.3 129.1 %copy-start.7 = (f32[384,768]{1,0:T(8,128)S(1)}, f32[384,768]{1,0:T(8,128)}, u32[]{:S(2)}) copy-start(f32[384,768]{1,0:T(8,128)} %param.20) | copy-start | bytes 3538948
  174.7 1.3 copy-start.5
  176.0 0.7 copy-start.11
  176.7 0.7 copy-start.13
  177.4 0.6 copy-start.15
  180.4 1.8 copy-start.2
  182.1 1.7 copy-start.3
  183.9 1.5 copy-start.6
  185.4 1.3 copy-start.8
  186.7 5.1 %copy-start.14 = (bf16[128,768]{1,0:T(8,128)(2,1)S(1)}, bf16[128,768]{1,0:T(8,128)(2,1)}, u32[]{:S(2)}) copy-start(bf16[128,768]{1,0:T(8,128)(2,1)} %copy-done.13) | copy-start | bytes 589828
  186.7 5.8 %copy-start.12 = (bf16[128,768]{1,0:T(8,128)(2,1)S(1)}, bf16[128,768]{1,0:T(8,128)(2,1)}, u32[]{:S(2)}) copy-start(bf16[128,768]{1,0:T(8,128)(2,1)} %copy-done.11) | copy-start | bytes 589828

commit v4 on v3

--- a/solution.py
+++ b/solution.py
@@ -184,14 +184,12 @@
 MAIN = DI + CHAN
 PADC = MAIN + 128
 T = 128
-PIECES = 4
 PR = 48
-CH = 8
-CW = 640
-SROWS = 24
+OUT_W = 384
+IN_W = 896
 MESH = pl.DeviceIdType.MESH
-VMEM_BYTES = 24 * 1024 * 1024
-LAYER_BYTES = 40 * 1024 * 1024
+VMEM_BYTES = 58 * 1024 * 1024
+LAYER_BYTES = VMEM_BYTES
 BF = jnp.bfloat16
 F32 = jnp.float32
 
@@ -298,17 +296,18 @@
 
 def layer_kernel(
     x_ref, ct_ref, len_ref, wi_ref, wo_own, par_ref,
-    out_ref, gx_ref, red, sm_out,
+    out_ref, gx_ref, red_out, red_in, sm_out,
     gate, ci, conv, inner, scan, mixes, dproj, tail, nt, n2t, gated, n16, dact,
-    dn2_all, dn2_out, out_part, out_in, d_own, d_in, n_in, n2_in, dp_in, own, half_in, rz, gs, sbuf, srecv,
-    s_o, r_o, s_w, r_w, s_d, r_d, s_n, r_n, s_2, r_2, s_p, r_p, s_h, r_h, s_z, r_z, s_g, r_g, s_x, r_x, s_s, r_s,
+    dn2_all, dn2_out, out_part, out_in, d_own, d_in, n_in, n2_in, dp_in, own_out, half_out, quart_out, last_out,
+    own_in, half_in, quart_in, last_in, gs, sbuf, srecv,
+    s_o, r_o, s_w, r_w, s_d, r_d, s_n, r_n, s_2, r_2, s_p, r_p, s_r, r_r, s_s, r_s,
 ):
     z, x_at, y, c = place()
     core, other_y = target(z, x_at, y, 1 - c), target(z, x_at, 1 - y, c)
     diag, other_x = target(z, x_at, 1 - y, 1 - c), target(z, 1 - x_at, y, c)
-    others = [lax.rem(z + d, 4) for d in (1, 2, 3)]
-    over_z = [target(o, x_at, y, c) for o in others]
-    greet([core, other_y, diag, other_x] + over_z)
+    low, high = lax.rem(z, 2), z // 2
+    near_z, far_z = target(2 * high + 1 - low, x_at, y, c), target(2 * (1 - high) + low, x_at, y, c)
+    greet([core, other_y, diag, other_x, near_z, far_z])
     started = []
 
     def go(*args):
@@ -454,6 +453,61 @@
             dlog = dlog + jnp.where(lane == h, jnp.sum(wide * srow, axis=1, keepdims=True), 0.0)
             parts.append(dot_tn((inter * decay * srow).astype(BF), ds16))
         dact[:, cols] = jnp.where(left, parts[0], parts[1]) + dscan * skip_of(q)
+    def total_of(lefts, rights, cols):
+        value = dot(lefts[0], rights[0][:, cols])
+        for a, b in zip(lefts[1:], rights[1:]):
+            value = value + dot(a, b[:, cols])
+        return value
+
+    class Piece:
+        def __init__(self, own, red, p, half, quart, last):
+            self.own, self.red, self.p = own, red, p
+            self.half, self.quart, self.last = half.at[p], quart.at[p], last.at[p]
+            self.sem = len(pieces_made)
+            pieces_made.append(self)
+
+        def go(self, step, src, dst, peer):
+            self.copy = go(src, dst, s_r.at[step, self.sem], r_r.at[step, self.sem], peer)
+
+        def add(self, dst, got):
+            self.copy.wait_recv()
+            for i in range(dst.shape[0]):
+                at = dst.at[i]
+                at[...] = (at[...].astype(F32) + got[i].astype(F32)).astype(BF)
+
+        def over_x(self):
+            self.go(0, self.own.at[1 - x_at, self.p], self.half, other_x)
+
+        def near(self):
+            mine = self.own.at[x_at, self.p]
+            self.add(mine, self.half)
+            self.go(1, mine.at[pl.ds(2 * (1 - low), 2)], self.quart, near_z)
+
+        def far(self):
+            mine = self.own.at[x_at, self.p]
+            self.add(mine.at[pl.ds(2 * low, 2)], self.quart)
+            self.go(2, mine.at[2 * low + 1 - high], self.last, far_z)
+
+        def back_far(self):
+            self.copy.wait_recv()
+            at = 2 * low + high
+            value = self.own[x_at, self.p, at].astype(F32) + self.last[...].astype(F32)
+            self.red[x_at, self.p, at] = value.astype(BF)
+            part = self.red.at[x_at, self.p, at]
+            self.go(3, part, part, far_z)
+
+        def back_near(self):
+            self.copy.wait_recv()
+            part = self.red.at[x_at, self.p, pl.ds(2 * low, 2)]
+            self.go(4, part, part, near_z)
+
+        def back_x(self):
+            self.copy.wait_recv()
+            part = self.red.at[x_at, self.p]
+            self.go(5, part, part, other_x)
+
+    pieces_made = []
+
     def spread_dproj(part, cols):
         return [
             go(dproj.at[:, cols], dp_in.at[i, :, cols], s_p.at[part, i], r_p.at[part, i], group[i][0])
@@ -461,11 +515,16 @@
         ]
 
     dp_got = [spread_dproj(0, pl.ds(0, DI))]
-    out_got = []
-    for i, (peer, shard) in enumerate(group):
-        n2_got[i].wait_recv()
-        out_part[i] = dot_tn(n2_in[i], wo_own[...]).astype(BF)
-        out_got.append(go(out_part.at[i], out_in.at[i], s_o.at[i], r_o.at[i], peer))
+    for copy in n2_got:
+        copy.wait_recv()
+    d_all = [d_own] + [d_in.at[i] for i in range(3)]
+    n2_all = [n2t[me]] + [n2_in[i] for i in range(3)]
+    for p in range(2):
+        value = total_of(n2_all, d_all, slice(OUT_W * p, OUT_W * p + OUT_W)).astype(BF)
+        own_out[:, p] = value.reshape(2, 4, PR, OUT_W)
+    steps = [Piece(own_out, red_out, p, half_out, quart_out, last_out) for p in range(2)]
+    for piece in steps:
+        piece.over_x()
     rest = jnp.zeros((T - HEADS, T), F32)
     dstep = jnp.concatenate(dstep_rows + [rest], axis=0).T
     dlog = dlog + jnp.concatenate(dlog_rows + [rest], axis=0).T
@@ -506,99 +565,69 @@
     gx_ref[...] = dx.astype(BF)
 
     small_copy = go(gs, srecv.at[0], s_s.at[0], r_s.at[0], core)
+    for piece in steps:
+        piece.near()
     forwarded = []
     for part, cols in enumerate((pl.ds(0, DI), pl.ds(DI, PADC - DI))):
         dp_got[part][1].wait_recv()
         forwarded.append(go(
             dp_in.at[1, :, cols], dp_in.at[2, :, cols], s_p.at[part, 2], r_p.at[part, 2], core
         ))
+    for piece in steps:
+        piece.far()
+    for part in range(2):
         dp_got[part][0].wait_recv()
     for copy in n_got:
         copy.wait_recv()
-    n_all = [nt[me]] + [n_in[i] for i in range(3)]
-    n2_all = [n2t[me]] + [n2_in[i] for i in range(3)]
-    d_all = [d_own] + [d_in.at[i] for i in range(3)]
-    dp_all = [dproj] + [dp_in.at[i] for i in range(3)]
-
-    def put(chunk, first, value):
-        wide = value.shape[1]
-        own[:, chunk, :, first:first + wide] = value.astype(BF).reshape(PIECES, PR, wide)
-
-    def total(lefts, rights, cols):
-        value = dot(lefts[0], rights[0][:, cols])
-        for a, b in zip(lefts[1:], rights[1:]):
-            value = value + dot(a, b[:, cols])
-        return value
-
-    rows_a, rows_b = [v[:192] for v in n2_all], [v[192:] for v in n2_all]
-    put(5, 256, total(rows_a, d_all, slice(0, 384)))
-    put(6, 0, total(rows_a, d_all, slice(384, 768)))
-    put(6, 384, total(rows_b, d_all, slice(0, 256)))
-    put(7, 0, total(rows_b, d_all, slice(256, 768)))
-    put(7, 512, jnp.zeros((192, 128), F32))
     small_copy.wait_recv()
     sbuf[0] = gs[...] + srecv[0]
     small_copy = go(sbuf.at[0], srecv.at[1], s_s.at[1], r_s.at[1], other_y)
+    for piece in steps:
+        piece.back_far()
+    n_all = [nt[me]] + [n_in[i] for i in range(3)]
+    dp_all = [dproj] + [dp_in.at[i] for i in range(3)]
+
+    def put(k, first, value):
+        wide = value.shape[1]
+        own_in[:, :, k, :, first:first + wide] = value.astype(BF).reshape(2, 2, PR, wide)
+
     forwarded[0].wait_recv()
-    for k in range(2):
-        put(k, 0, total(n_all, dp_all, slice(CW * k, CW * k + CW)))
+    put(0, 0, total_of(n_all, dp_all, slice(0, IN_W)))
     forwarded[1].wait_recv()
-    for k in range(2, 5):
-        put(k, 0, total(n_all, dp_all, slice(CW * k, CW * k + CW)))
-    put(5, 0, total(n_all, dp_all, slice(5 * CW, PADC)))
-
-    mine, away = pl.ds(4 * x_at, 4), pl.ds(4 * (1 - x_at), 4)
-    halves = [go(own.at[p, away], half_in.at[p], s_h.at[p], r_h.at[p], other_x) for p in range(PIECES)]
-    small_copy.wait_recv()
-    sbuf[1] = sbuf[0] + srecv[1]
-    small_copy = go(sbuf.at[1], srecv.at[2], s_s.at[2], r_s.at[2], other_x)
-    spread = []
-    for p in range(PIECES):
-        halves[p].wait_recv()
-        for i in range(4):
-            at = own.at[p, 4 * x_at + i]
-            at[...] = (at[...].astype(F32) + half_in[p, i].astype(F32)).astype(BF)
-        spread.append([
-            go(own.at[p, 4 * x_at + others[d]], rz.at[p, d], s_z.at[p, d], r_z.at[p, d], over_z[d])
-            for d in range(3)
-        ])
-    small_copy.wait_recv()
-    sbuf[2] = sbuf[1] + srecv[2]
-    small = [go(sbuf.at[2], srecv.at[3 + d], s_s.at[3 + d], r_s.at[3 + d], over_z[d]) for d in range(3)]
-    back = []
-    for p in range(PIECES):
-        for copy in spread[p]:
-            copy.wait_recv()
-        value = own[p, 4 * x_at + z].astype(F32)
-        for d in range(3):
-            value = value + rz[p, d].astype(F32)
-        at = red.at[p, 4 * x_at + z]
-        at[...] = value.astype(BF)
-        back.append([go(at, at, s_g.at[p, d], r_g.at[p, d], over_z[d]) for d in range(3)])
-    last = []
-    for p in range(PIECES):
-        for copy in back[p]:
-            copy.wait_recv()
-        at = red.at[p, mine]
-        last.append(go(at, at, s_x.at[p], r_x.at[p], other_x))
-    for copy in small:
-        copy.wait_recv()
-    pieces = [sbuf[2], srecv[3], srecv[4], srecv[5]]
-    value = jnp.zeros(gs.shape, F32)
-    for zi in range(4):
-        back_by = lax.rem(z - zi + 4, 4)
-        pick = pieces[0]
-        for d in (1, 2, 3):
-            pick = jnp.where(back_by == d, pieces[d], pick)
-        value = value + pick
-    sm_out[...] = value
+    for k in range(1, 3):
+        put(k, 0, total_of(n_all, dp_all, slice(IN_W * k, IN_W * k + IN_W)))
+    put(3, 0, total_of(n_all, dp_all, slice(IN_W * 3, PADC)))
+    put(3, PADC - 3 * IN_W, jnp.zeros((192, 4 * IN_W - PADC), F32))
+    main = [Piece(own_in, red_in, p, half_in, quart_in, last_in) for p in range(2)]
+    for piece in main:
+        piece.over_x()
+    for piece in steps:
+        piece.back_near()
+    out_got = []
+    for i, (peer, shard) in enumerate(group):
+        out_part[i] = dot_tn(n2_in[i], wo_own[...]).astype(BF)
+        out_got.append(go(out_part.at[i], out_in.at[i], s_o.at[i], r_o.at[i], peer))
+    for s, (peer, piece_step) in enumerate(((other_x, "near"), (near_z, "far"), (far_z, "back_far"))):
+        for piece in main:
+            getattr(piece, piece_step)()
+        small_copy.wait_recv()
+        sbuf[s + 1] = sbuf[s] + srecv[s + 1]
+        small_copy = go(sbuf.at[s + 1], srecv.at[s + 2], s_s.at[s + 2], r_s.at[s + 2], peer)
+    for piece in steps:
+        piece.back_x()
+    for piece in main:
+        piece.back_near()
     out = x_ref[...].astype(F32) + dot_tn(n2t[me], wo_own[...])
     for i in range(3):
         out_got[i].wait_recv()
         out = out + out_in[i].astype(F32)
     out_ref[...] = out.astype(BF)
-    for copy in last:
-        copy.wait_recv()
+    for piece in main:
+        piece.back_x()
+    small_copy.wait_recv()
+    sm_out[...] = sbuf[3] + srecv[4]
+    for piece in steps + main:
+        piece.copy.wait_recv()
     for copy in started:
         copy.wait_send()
 
@@ -610,10 +639,11 @@
     return pl.pallas_call(
         layer_kernel,
         out_shape=(
-            shape((T, D), BF), shape((T, D), BF), shape((PIECES, CH, PR, CW), BF), shape((8, CHAN), F32),
+            shape((T, D), BF), shape((T, D), BF), shape((2, 2, 4, PR, OUT_W), BF),
+            shape((2, 2, 4, PR, IN_W), BF), shape((8, CHAN), F32),
         ),
         in_specs=[vmem, vmem, pl.BlockSpec(memory_space=pltpu.SMEM)] + [vmem] * 3,
-        out_specs=[vmem] * 4,
+        out_specs=[vmem] * 5,
         scratch_shapes=[
             pltpu.VMEM((T, DI), F32), pltpu.VMEM((T, CHAN), F32), pltpu.VMEM((T, CHAN), F32),
             pltpu.VMEM((T, CHAN), BF), pltpu.VMEM((T, DI), F32), pltpu.VMEM((HEADS, T, T), F32),
@@ -623,12 +653,13 @@
             pltpu.VMEM((4, T, 384), BF), pltpu.VMEM((3, T, 384), BF), pltpu.VMEM((3, T, D), BF),
             pltpu.VMEM((3, T, D), BF), pltpu.VMEM((T, D), BF), pltpu.VMEM((3, T, D), BF),
             pltpu.VMEM((3, 192, T), BF), pltpu.VMEM((3, 384, T), BF), pltpu.VMEM((3, T, PADC), BF),
-            pltpu.VMEM((PIECES, CH, PR, CW), BF), pltpu.VMEM((PIECES, 4, PR, CW), BF),
-            pltpu.VMEM((PIECES, 3, PR, CW), BF), pltpu.VMEM((8, CHAN), F32),
-            pltpu.VMEM((3, 8, CHAN), F32), pltpu.VMEM((6, 8, CHAN), F32),
+            pltpu.VMEM((2, 2, 4, PR, OUT_W), BF), pltpu.VMEM((2, 4, PR, OUT_W), BF),
+            pltpu.VMEM((2, 2, PR, OUT_W), BF), pltpu.VMEM((2, PR, OUT_W), BF),
+            pltpu.VMEM((2, 2, 4, PR, IN_W), BF), pltpu.VMEM((2, 4, PR, IN_W), BF),
+            pltpu.VMEM((2, 2, PR, IN_W), BF), pltpu.VMEM((2, PR, IN_W), BF),
+            pltpu.VMEM((8, CHAN), F32), pltpu.VMEM((4, 8, CHAN), F32), pltpu.VMEM((5, 8, CHAN), F32),
             dma((3,)), dma((3,)), dma((3,)), dma((3,)), dma((3,)), dma((3,)), dma((3,)), dma((3,)), dma((3,)), dma((3,)),
-            dma((2, 3)), dma((2, 3)), dma((PIECES,)), dma((PIECES,)), dma((PIECES, 3)), dma((PIECES, 3)),
-            dma((PIECES, 3)), dma((PIECES, 3)), dma((PIECES,)), dma((PIECES,)), dma((6,)), dma((6,)),
+            dma((2, 3)), dma((2, 3)), dma((6, 4)), dma((6, 4)), dma((5,)), dma((5,)),
         ],
         compiler_params=pltpu.CompilerParams(
             collective_id=1, has_side_effects=True, vmem_limit_bytes=LAYER_BYTES
@@ -637,9 +668,9 @@
     )(tokens, cotangent, lens, w_in, w_out, params)
 
 
-def adamw_kernel(red, wi, mi, vi, wo, mo, vo, nwi, nmi, nvi, nwo, nmo, nvo):
-    def update(cols, grad, refs, rate, part=None):
-        at = (slice(None), cols) if part is None else (part, slice(None), cols)
+def adamw_kernel(red_out, red_in, wi, mi, vi, wo, mo, vo, nwi, nmi, nvi, nwo, nmo, nvo):
+    def update(cols, grad, refs, rate, part):
+        at = (part, cols)
         gradient, master = grad.astype(F32), refs[0][at].astype(F32)
         first = beta_one * refs[1][at] + (1.0 - beta_one) * gradient
         second = beta_two * refs[2][at] + (1.0 - beta_two) * gradient * gradient
@@ -651,31 +682,32 @@
 
     refs_in = (wi, mi, vi, nwi, nmi, nvi)
     refs_out = (wo, mo, vo, nwo, nmo, nvo)
-    for k in range(5):
-        update(slice(CW * k, CW * k + CW), red[0, k], refs_in, 0.05)
-    update(slice(5 * CW, CIN), red[0, 5, :, :CIN - 5 * CW], refs_in, 0.05)
-    update(slice(0, 384), red[0, 5, :, 256:], refs_out, 0.04, 0)
-    update(slice(384, 768), red[0, 6, :, :384], refs_out, 0.04, 0)
-    update(slice(0, 256), red[0, 6, :, 384:], refs_out, 0.04, 1)
-    update(slice(256, 768), red[0, 7, :, :512], refs_out, 0.04, 1)
-
-
-def adamw_all(red, w_in, m_in, v_in, w_out, m_out, v_out):
-    rows = PR
-    halves = [v.reshape(2, 192, D) for v in (w_out, m_out, v_out)]
-    spec_in = pl.BlockSpec((rows, CIN), lambda i: (i, 0))
-    spec_out = pl.BlockSpec((2, rows, D), lambda i: (0, i, 0))
-    new = pl.pallas_call(
+    for k in range(4):
+        wide = min(IN_W, CIN - IN_W * k)
+        update(slice(IN_W * k, IN_W * k + wide), red_in[0, 0, k, :, :wide], refs_in, 0.05, slice(None))
+    for p in range(2):
+        for k in range(2):
+            update(
+                slice(OUT_W * p, OUT_W * p + OUT_W), red_out[0, p, k], refs_out, 0.04,
+                slice(PR * k, PR * k + PR),
+            )
+
+
+def adamw_all(red_out, red_in, w_in, m_in, v_in, w_out, m_out, v_out):
+    spec_in = pl.BlockSpec((PR, CIN), lambda i: (i, 0))
+    spec_out = pl.BlockSpec((2 * PR, D), lambda i: (i, 0))
+    return pl.pallas_call(
         adamw_kernel,
-        grid=(192 // rows,),
-        out_shape=[jax.ShapeDtypeStruct((192, CIN), F32)] * 3 + [jax.ShapeDtypeStruct((2, 192, D), F32)] * 3,
-        in_specs=[pl.BlockSpec((1, CH, rows, CW), lambda i: (i, 0, 0, 0))]
-        + [spec_in] * 3 + [spec_out] * 3,
+        grid=(4,),
+        out_shape=[jax.ShapeDtypeStruct((192, CIN), F32)] * 3 + [jax.ShapeDtypeStruct((384, D), F32)] * 3,
+        in_specs=[
+            pl.BlockSpec((1, 2, 2, PR, OUT_W), lambda i: (i // 2, 0, i % 2, 0, 0)),
+            pl.BlockSpec((1, 1, 4, PR, IN_W), lambda i: (i // 2, i % 2, 0, 0, 0)),
+        ] + [spec_in] * 3 + [spec_out] * 3,
         out_specs=[spec_in] * 3 + [spec_out] * 3,
         compiler_params=pltpu.CompilerParams(vmem_limit_bytes=VMEM_BYTES),
         name="adamw",
-    )(red, w_in, m_in, v_in, *halves)
-    return list(new[:3]) + [v.reshape(384, D) for v in new[3:]]
+    )(red_out, red_in, w_in, m_in, v_in, w_out, m_out, v_out)
 
 
 def on_device_fast(
@@ -692,7 +724,7 @@
         packed[:start], packed[gains : gains + D], heads.reshape(-1), jnp.zeros(CHAN - D - 384, F32),
         packed[gains + D :], jnp.zeros(2 * CHAN - DI, F32),
     ]).reshape(8, CHAN)
-    out, gx, red, sums = layer(
+    out, gx, red_out, red_in, sums = layer(
         tokens, cotangent, seq_lengths, full_in.reshape(D, CIN), w_out, params
     )
     flat = jnp.concatenate([
@@ -700,7 +732,7 @@
         sums[5, D + 256 : D + 256 + HEADS], sums[5, :D], sums[6, :DI],
     ])
     share_small = lax.dynamic_slice_in_dim(flat, lax.axis_index("shard") * share, share)
-    new = adamw_all(red, w_in, m_in, v_in, w_out, m_out, v_out)
+    new = adamw_all(red_out, red_in, w_in, m_in, v_in, w_out, m_out, v_out)
     new_small = adamw(w_small, share_small, m_small, v_small, 0.3, 0.0)
     return (out, gx, *new, *new_small)
 

time: 194 us -> 175 us (0.902)
  local copies, waits for them, and re-layouts: 17.5 us -> 7.61 us
  Pallas kernels: 173 us -> 165 us
    unnamed x44 -> x18, local copies, waits for them, and re-layouts: 15 us -> 2.33 us
    pallas_call x1, Pallas kernels: 123 us -> 111 us  [layer(): pl.pallas_call(layer_kernel, out_shape=(shape((T, D), BF), shape((T, D),...]
    pallas_call x1, Pallas kernels: 5.12 us -> 9.28 us  [adamw_all(): pl.pallas_call(adamw_kernel, grid=(4,), out_shape=[jax.ShapeDtypeStruct((...]
where the time goes in v4:
time: 175 us; the launch traced here: 174 us
  Pallas kernels  165 us (94%)
  local copies, waits for them, and re-layouts  7.61 us (4%)
    pallas_call x1, Pallas kernels, layer(): pl.pallas_call(layer_kernel, out_shape=(shape((T, D), BF), shape((T, D),...  111 us
    pallas_call x1, Pallas kernels, gather_weights(): pl.pallas_call(gather_kernel, out_shape=(jax.ShapeDtypeStruct((4, 192, CI...  44.9 us
    pallas_call x1, Pallas kernels, adamw_all(): pl.pallas_call(adamw_kernel, grid=(4,), out_shape=[jax.ShapeDtypeStruct((...  9.28 us

profile of v4, /device:TPU:0, one launch (start us, length us, event | category | flops | bytes accessed | tf_op | source)
XLA Modules:
  0.0 174.2 jit_solution(14977685446522037320)
XLA Ops:
  0.6 1.3 pad_bitcast_fusion.sm
  1.9 44.9 %gather_weights.1 = (bf16[4,192,3352]{2,1,0:T(8,128)(2,1)}, bf16[4,32,128]{2,1,0:T(8,128)(2,1)}) custom-call(bf16[192,3352]{1,0:T(8,128)(2,1)} %wi.3, bf16[32,128]{1,0:T(8,128)(2,1)} %pad_bitcast_fusion.sm), custom_call_target="tpu_custom_call" | custom-call | tf_op jit(solution)/shard_map/gather_weights/pallas_call | solution.py:266
  46.8 0.8 copy.25
  47.6 0.1 reshape.53
  47.7 0.1 slice_dynamic-update-slice_fusion.2
  47.8 0.1 reshape.49
  47.9 0.1 slice_dynamic-update-slice_fusion.1
  48.0 0.6 reshape.51.par_ref
  48.6 0.0 copy-start.2
  48.6 111.0 %layer.1 = (bf16[128,768]{1,0:T(8,128)(2,1)}, bf16[128,768]{1,0:T(8,128)(2,1)}, bf16[2,2,4,48,384]{4,3,2,1,0:T(8,128)(2,1)}, bf16[2,2,4,48,896]{4,3,2,1,0:T(8,128)(2,1)}, f32[8,1792]{1,0:T(8,128)}) custom-call(bf16[128,768]{1,0:T(8,128)(2,1)} %x_ref.1, bf16[128,768]{1,0:T(8,128)(2,1)} %ct_ref.1, s32[1,4]{1,0:T(1,128)} %len_ref.1, ...), custom_call_target="tpu_custom_call" | custom-call | tf_op jit(solution)/shard_map/layer/pallas_call | solution.py:639
  159.6 0.7 slice_bitcast_fusion
  160.3 0.8 slice_reduce_fusion.1
  161.1 0.8 slice_reduce_fusion
  161.9 0.8 reshape.52
  162.7 0.1 concatenate.7
  162.8 0.0 copy-done.2
  162.8 0.0 copy-done.3
  162.8 0.0 copy-done.4
  162.8 0.7 convert_subtract_fusion
  163.5 9.3 %adamw.1 = (f32[192,3352]{1,0:T(8,128)}, f32[192,3352]{1,0:T(8,128)}, f32[192,3352]{1,0:T(8,128)}, f32[384,768]{1,0:T(8,128)}, f32[384,768]{1,0:T(8,128)}, /*index=5*/f32[384,768]{1,0:T(8,128)}) custom-call(bf16[2,2,4,48,384]{4,3,2,1,0:T(8,128)(2,1)} %get-tuple-element.28.red_out, bf16[2,2,4,48,896]{4,3,2,1,0:T(8,128)(2,1)} %get-tuple-element.29.red_in, ...), custom_call_target="tpu_custom_call" | custom-call | tf_op jit(solution)/shard_map/adamw/pallas_call | solution.py:699
  172.8 0.0 copy-done.1
  172.8 0.7 copy.34
  173.5 0.0 copy-done
  173.5 0.7 copy.35
  (11 shorter events, 0.0 us)
Async XLA Ops:
  48.6 114.2 %copy-start.2 = (bf16[2834]{0:T(1024)(128)(2,1)S(1)}, bf16[2834]{0:T(1024)(128)(2,1)}, u32[]{:S(2)}) copy-start(bf16[2834]{0:T(1024)(128)(2,1)} %param.17) | copy-start | bytes 17008
  48.6 114.2 %copy-start.3 = (f32[2834]{0:T(1024)S(1)}, f32[2834]{0:T(1024)}, u32[]{:S(2)}) copy-start(f32[2834]{0:T(1024)} %param.22) | copy-start | bytes 34012
  48.6 114.2 %copy-start.4 = (f32[2834]{0:T(1024)S(1)}, f32[2834]{0:T(1024)}, u32[]{:S(2)}) copy-start(f32[2834]{0:T(1024)} %param.23) | copy-start | bytes 34012
  163.5 9.3 %copy-start.1 = (bf16[128,768]{1,0:T(8,128)(2,1)S(1)}, bf16[128,768]{1,0:T(8,128)(2,1)}, u32[]{:S(2)}) copy-start(bf16[128,768]{1,0:T(8,128)(2,1)} %get-tuple-element.54) | copy-start | bytes 589828
  163.5 10.0 %copy-start = (bf16[128,768]{1,0:T(8,128)(2,1)S(1)}, bf16[128,768]{1,0:T(8,128)(2,1)}, u32[]{:S(2)}) copy-start(bf16[128,768]{1,0:T(8,128)(2,1)} %get-tuple-element.55) | copy-start | bytes 589828

commit v5 on v4

--- a/solution.py
+++ b/solution.py
@@ -466,45 +466,88 @@
             self.sem = len(pieces_made)
             pieces_made.append(self)
 
-        def go(self, step, src, dst, peer):
-            self.copy = go(src, dst, s_r.at[step, self.sem], r_r.at[step, self.sem], peer)
+        def go(self, step, peer, *pairs):
+            self.copies = [
+                go(src, dst, s_r.at[step, self.sem, i], r_r.at[step, self.sem, i], peer)
+                for i, (src, dst) in enumerate(pairs)
+            ]
+
+        def arrive(self):
+            for copy in self.copies:
+                copy.wait_recv()
 
         def add(self, dst, got):
-            self.copy.wait_recv()
             for i in range(dst.shape[0]):
                 at = dst.at[i]
                 at[...] = (at[...].astype(F32) + got[i].astype(F32)).astype(BF)
 
-        def over_x(self):
-            self.go(0, self.own.at[1 - x_at, self.p], self.half, other_x)
-
-        def near(self):
-            mine = self.own.at[x_at, self.p]
-            self.add(mine, self.half)
-            self.go(1, mine.at[pl.ds(2 * (1 - low), 2)], self.quart, near_z)
-
-        def far(self):
-            mine = self.own.at[x_at, self.p]
-            self.add(mine.at[pl.ds(2 * low, 2)], self.quart)
-            self.go(2, mine.at[2 * low + 1 - high], self.last, far_z)
-
-        def back_far(self):
-            self.copy.wait_recv()
+        def finish(self, peer):
             at = 2 * low + high
             value = self.own[x_at, self.p, at].astype(F32) + self.last[...].astype(F32)
             self.red[x_at, self.p, at] = value.astype(BF)
             part = self.red.at[x_at, self.p, at]
-            self.go(3, part, part, far_z)
+            self.go(3, peer, (part, part))
+
+        def share(self, step, peer, *parts):
+            self.arrive()
+            self.go(step, peer, *[(part, part) for part in parts])
+
+    class XFirst(Piece):
+        def over_x(self):
+            self.go(0, other_x, (self.own.at[1 - x_at, self.p], self.half))
+
+        def near(self):
+            mine = self.own.at[x_at, self.p]
+            self.arrive()
+            self.add(mine, self.half)
+            self.go(1, near_z, (mine.at[pl.ds(2 * (1 - low), 2)], self.quart))
+
+        def far(self):
+            mine = self.own.at[x_at, self.p]
+            self.arrive()
+            self.add(mine.at[pl.ds(2 * low, 2)], self.quart)
+            self.go(2, far_z, (mine.at[2 * low + 1 - high], self.last))
+
+        def back_far(self):
+            self.arrive()
+            self.finish(far_z)
 
         def back_near(self):
-            self.copy.wait_recv()
-            part = self.red.at[x_at, self.p, pl.ds(2 * low, 2)]
-            self.go(4, part, part, near_z)
+            self.share(4, near_z, self.red.at[x_at, self.p, pl.ds(2 * low, 2)])
 
         def back_x(self):
-            self.copy.wait_recv()
-            part = self.red.at[x_at, self.p]
-            self.go(5, part, part, other_x)
+            self.share(5, other_x, self.red.at[x_at, self.p])
+
+    class ZFirst(Piece):
+        def over_x(self):
+            away = pl.ds(2 * (1 - low), 2)
+            self.go(0, near_z, *[
+                (self.own.at[i, self.p, away], self.half.at[pl.ds(2 * i, 2)]) for i in range(2)
+            ])
+
+        def near(self):
+            self.arrive()
+            for i in range(2):
+                self.add(self.own.at[i, self.p, pl.ds(2 * low, 2)], self.half.at[pl.ds(2 * i, 2)])
+            away = 2 * low + 1 - high
+            self.go(1, far_z, *[(self.own.at[i, self.p, away], self.quart.at[i]) for i in range(2)])
+
+        def far(self):
+            self.arrive()
+            at = 2 * low + high
+            for i in range(2):
+                self.add(self.own.at[i, self.p, pl.ds(at, 1)], self.quart.at[pl.ds(i, 1)])
+            self.go(2, other_x, (self.own.at[1 - x_at, self.p, at], self.last))
+
+        def back_far(self):
+            self.arrive()
+            self.finish(other_x)
+
+        def back_near(self):
+            self.share(4, far_z, *[self.red.at[i, self.p, 2 * low + high] for i in range(2)])
+
+        def back_x(self):
+            self.share(5, near_z, *[self.red.at[i, self.p, pl.ds(2 * low, 2)] for i in range(2)])
 
     pieces_made = []
 
@@ -522,7 +565,10 @@
     for p in range(2):
         value = total_of(n2_all, d_all, slice(OUT_W * p, OUT_W * p + OUT_W)).astype(BF)
         own_out[:, p] = value.reshape(2, 4, PR, OUT_W)
-    steps = [Piece(own_out, red_out, p, half_out, quart_out, last_out) for p in range(2)]
+    steps = [
+        kind(own_out, red_out, p, half_out, quart_out, last_out)
+        for p, kind in enumerate((XFirst, ZFirst))
+    ]
     for piece in steps:
         piece.over_x()
     rest = jnp.zeros((T - HEADS, T), F32)
@@ -598,7 +644,10 @@
         put(k, 0, total_of(n_all, dp_all, slice(IN_W * k, IN_W * k + IN_W)))
     put(3, 0, total_of(n_all, dp_all, slice(IN_W * 3, PADC)))
     put(3, PADC - 3 * IN_W, jnp.zeros((192, 4 * IN_W - PADC), F32))
-    main = [Piece(own_in, red_in, p, half_in, quart_in, last_in) for p in range(2)]
+    main = [
+        kind(own_in, red_in, p, half_in, quart_in, last_in)
+        for p, kind in enumerate((XFirst, ZFirst))
+    ]
     for piece in main:
         piece.over_x()
     for piece in steps:
@@ -627,7 +676,7 @@
     small_copy.wait_recv()
     sm_out[...] = sbuf[3] + srecv[4]
     for piece in steps + main:
-        piece.copy.wait_recv()
+        piece.arrive()
     for copy in started:
         copy.wait_send()
 
@@ -659,7 +708,7 @@
             pltpu.VMEM((2, 2, PR, IN_W), BF), pltpu.VMEM((2, PR, IN_W), BF),
             pltpu.VMEM((8, CHAN), F32), pltpu.VMEM((4, 8, CHAN), F32), pltpu.VMEM((5, 8, CHAN), F32),
             dma((3,)), dma((3,)), dma((3,)), dma((3,)), dma((3,)), dma((3,)), dma((3,)), dma((3,)), dma((3,)), dma((3,)),
-            dma((2, 3)), dma((2, 3)), dma((6, 4)), dma((6, 4)), dma((5,)), dma((5,)),
+            dma((2, 3)), dma((2, 3)), dma((6, 4, 2)), dma((6, 4, 2)), dma((5,)), dma((5,)),
         ],
         compiler_params=pltpu.CompilerParams(
             collective_id=1, has_side_effects=True, vmem_limit_bytes=LAYER_BYTES

time: 175 us -> 167 us (0.954)
  Pallas kernels: 165 us -> 158 us
    pallas_call x1, Pallas kernels: 111 us -> 104 us  [layer(): pl.pallas_call(layer_kernel, out_shape=(shape((T, D), BF), shape((T, D),...]
where the time goes in v5:
time: 167 us
  Pallas kernels  158 us (95%)
  local copies, waits for them, and re-layouts  7.61 us (5%)
    pallas_call x1, Pallas kernels, layer(): pl.pallas_call(layer_kernel, out_shape=(shape((T, D), BF), shape((T, D),...  104 us
    pallas_call x1, Pallas kernels, gather_weights(): pl.pallas_call(gather_kernel, out_shape=(jax.ShapeDtypeStruct((4, 192, CI...  44.9 us
    pallas_call x1, Pallas kernels, adamw_all(): pl.pallas_call(adamw_kernel, grid=(4,), out_shape=[jax.ShapeDtypeStruct((...  9.28 us

profile of v5, /device:TPU:0, one launch (start us, length us, event | category | flops | bytes accessed | tf_op | source)
XLA Modules:
  0.0 167.0 jit_solution(17713321027556839874)
XLA Ops:
  0.6 1.3 pad_bitcast_fusion.sm
  1.9 44.9 %gather_weights.1 = (bf16[4,192,3352]{2,1,0:T(8,128)(2,1)}, bf16[4,32,128]{2,1,0:T(8,128)(2,1)}) custom-call(bf16[192,3352]{1,0:T(8,128)(2,1)} %wi.3, bf16[32,128]{1,0:T(8,128)(2,1)} %pad_bitcast_fusion.sm), custom_call_target="tpu_custom_call" | custom-call | tf_op jit(solution)/shard_map/gather_weights/pallas_call | solution.py:266
  46.8 0.8 copy.25
  47.6 0.1 reshape.53
  47.7 0.1 slice_dynamic-update-slice_fusion.2
  47.8 0.1 reshape.49
  47.9 0.1 slice_dynamic-update-slice_fusion.1
  48.0 0.6 reshape.51.par_ref
  48.6 0.0 copy-start.2
  48.6 103.8 %layer.1 = (bf16[128,768]{1,0:T(8,128)(2,1)}, bf16[128,768]{1,0:T(8,128)(2,1)}, bf16[2,2,4,48,384]{4,3,2,1,0:T(8,128)(2,1)}, bf16[2,2,4,48,896]{4,3,2,1,0:T(8,128)(2,1)}, f32[8,1792]{1,0:T(8,128)}) custom-call(bf16[128,768]{1,0:T(8,128)(2,1)} %x_ref.1, bf16[128,768]{1,0:T(8,128)(2,1)} %ct_ref.1, s32[1,4]{1,0:T(1,128)} %len_ref.1, ...), custom_call_target="tpu_custom_call" | custom-call | tf_op jit(solution)/shard_map/layer/pallas_call | solution.py:688
  152.4 0.7 slice_bitcast_fusion
  153.1 0.8 slice_reduce_fusion.1
  153.8 0.8 slice_reduce_fusion
  154.7 0.8 reshape.52
  155.5 0.1 concatenate.7
  155.6 0.0 copy-done.2
  155.6 0.0 copy-done.3
  155.6 0.0 copy-done.4
  155.6 0.7 convert_subtract_fusion
  156.3 9.3 %adamw.1 = (f32[192,3352]{1,0:T(8,128)}, f32[192,3352]{1,0:T(8,128)}, f32[192,3352]{1,0:T(8,128)}, f32[384,768]{1,0:T(8,128)}, f32[384,768]{1,0:T(8,128)}, /*index=5*/f32[384,768]{1,0:T(8,128)}) custom-call(bf16[2,2,4,48,384]{4,3,2,1,0:T(8,128)(2,1)} %get-tuple-element.28.red_out, bf16[2,2,4,48,896]{4,3,2,1,0:T(8,128)(2,1)} %get-tuple-element.29.red_in, ...), custom_call_target="tpu_custom_call" | custom-call | tf_op jit(solution)/shard_map/adamw/pallas_call | solution.py:748
  165.6 0.0 copy-done.1
  165.6 0.7 copy.34
  166.3 0.0 copy-done
  166.3 0.7 copy.35
  (11 shorter events, 0.0 us)
Async XLA Ops:
  48.6 107.0 %copy-start.2 = (bf16[2834]{0:T(1024)(128)(2,1)S(1)}, bf16[2834]{0:T(1024)(128)(2,1)}, u32[]{:S(2)}) copy-start(bf16[2834]{0:T(1024)(128)(2,1)} %param.17) | copy-start | bytes 17008
  48.6 107.0 %copy-start.3 = (f32[2834]{0:T(1024)S(1)}, f32[2834]{0:T(1024)}, u32[]{:S(2)}) copy-start(f32[2834]{0:T(1024)} %param.22) | copy-start | bytes 34012
  48.6 107.0 %copy-start.4 = (f32[2834]{0:T(1024)S(1)}, f32[2834]{0:T(1024)}, u32[]{:S(2)}) copy-start(f32[2834]{0:T(1024)} %param.23) | copy-start | bytes 34012
  156.3 9.3 %copy-start.1 = (bf16[128,768]{1,0:T(8,128)(2,1)S(1)}, bf16[128,768]{1,0:T(8,128)(2,1)}, u32[]{:S(2)}) copy-start(bf16[128,768]{1,0:T(8,128)(2,1)} %get-tuple-element.54) | copy-start | bytes 589828
  156.3 10.0 %copy-start = (bf16[128,768]{1,0:T(8,128)(2,1)S(1)}, bf16[128,768]{1,0:T(8,128)(2,1)}, u32[]{:S(2)}) copy-start(bf16[128,768]{1,0:T(8,128)(2,1)} %get-tuple-element.55) | copy-start | bytes 589828
